TPU v7x, 32 devices: a whole 2x2x4 slice. The times are simulated.
32 devices in a mesh: groups: 2 (over x), seq: 8 (over z, y), head: 2 (over core).
Axes of the slice: x: 2, y: 2, z: 4, core: 2. Of those that a mesh axis runs over, the one named last changes fastest.
Arguments:
- query_rows: bfloat16 [2048, 4096], P(('groups', 'seq'), 'head'), parts along dimension 0, may hold values from -160 to 160
- key_rows: bfloat16 [2048, 512], P(('groups', 'seq'), 'head'), parts along dimension 0, may hold values from -6 to 6
- value_rows: bfloat16 [2048, 512], P(('groups', 'seq'), 'head'), parts along dimension 0, may hold values from -6 to 6
- grad_out: bfloat16 [2048, 4096], P(('groups', 'seq'), 'head'), parts along dimension 0, may hold values from -6 to 6
- lengths: int32 [64], P(('groups', 'seq')), parts along dimension 0, may hold values from 1 to 640, as said below
Outputs:
- attended: bfloat16 [2048, 4096], P(('groups', 'seq'), 'head'), parts along dimension 0
- grad_query: bfloat16 [2048, 4096], P(('groups', 'seq'), 'head'), parts along dimension 0
- grad_key: bfloat16 [2048, 512], P(('groups', 'seq'), 'head'), parts along dimension 0
- grad_value: bfloat16 [2048, 512], P(('groups', 'seq'), 'head'), parts along dimension 0
There are 2 independent parts, one for each index of `groups`. A program takes and returns all parts, laid end to end along the dimension named above; each array names one. Nothing has to cross between parts.
Inputs may be any that keep to these rules, and one draw needn't show every extreme that they name: The 32 lengths sum to 1024; the first document is the longest, with exactly 640 tokens.
All inputs are finite; a program needn't handle non-finite values.
Results may differ from a plain program's by a relative error of at most 0.035.
Values may be sent and summed in bfloat16 or wider, within the bound.
A program may use at most 64 MiB of HBM per device.

v0:
```python
import math

import jax
import jax.numpy as jnp
from jax import lax
from jax.sharding import PartitionSpec as P

HD = 128


NEGATIVE = -1e30


def from_behind(value, axis, steps):
    count = lax.axis_size(axis)
    leading, last = (max(0, -steps), min(count, count - steps))
    return lax.ppermute(value, axis, [(source, source + steps) for source in range(leading, last)])


def for_sending(shard):
    return jax.tree.map(lambda a: a.astype(jnp.bfloat16) if a.dtype == jnp.float32 else a, shard)


def doc_index(ends, positions):
    return jnp.sum((ends[None, :] <= positions[:, None]).astype(jnp.int32), axis=1)


def block_mask(ends, query_pos, query_docs, key_pos):
    key_docs = doc_index(ends, key_pos)
    return (
        (query_docs[:, None] == key_docs[None, :])
        & (key_pos[None, :] <= query_pos[:, None])
        & (key_pos[None, :] >= 0)
    )


def needed(ends, query_pos, query_docs, key_first, block):
    key_last = key_first + block - 1
    last_doc = jnp.sum((ends <= key_last).astype(jnp.int32))
    return (key_first <= query_pos[-1]) & (key_last >= 0) & (last_doc >= query_docs[0])


def tile_scores(query_four, key_block, scale):
    return scale * jnp.einsum(
        "tagd,kad->tagk", query_four, key_block, preferred_element_type=jnp.float32
    )


def forward_block(state, query_four, key_block, value_block, allowed, scale):
    rowmax, rowsum, accum = state
    scores = tile_scores(query_four, key_block, scale)
    allowed = allowed[:, None, None, :]
    masked = jnp.where(allowed, scores, NEGATIVE)
    new_max = jnp.maximum(rowmax, jnp.max(masked, axis=-1))
    expo = jnp.where(allowed, jnp.exp(masked - new_max[..., None]), 0.0)
    factor = jnp.exp(rowmax - new_max)
    rowsum = rowsum * factor + jnp.sum(expo, axis=-1)
    update = jnp.einsum(
        "tagk,kad->tagd", expo.astype(jnp.bfloat16), value_block, preferred_element_type=jnp.float32
    )
    accum = accum * factor[..., None] + update
    return (new_max, rowsum, accum)


def backward_block(back, key_block, value_block, allowed):
    query_four, grad_four, lse, delta, query_pos, query_docs, ends, scale = back
    scores = tile_scores(query_four, key_block, scale)
    allowed = allowed[:, None, None, :]
    masked = jnp.where(allowed, scores, NEGATIVE)
    prob = jnp.where(allowed, jnp.exp(masked - lse[..., None]), 0.0)
    value_part = jnp.einsum(
        "tagk,tagd->kad", prob.astype(jnp.bfloat16), grad_four, preferred_element_type=jnp.float32
    )
    dprob = jnp.einsum("tagd,kad->tagk", grad_four, value_block, preferred_element_type=jnp.float32)
    dscore = (prob * (dprob - delta[..., None])).astype(jnp.bfloat16)
    query_part = jnp.einsum("tagk,kad->tagd", dscore, key_block, preferred_element_type=jnp.float32)
    key_part = jnp.einsum("tagk,tagd->kad", dscore, query_four, preferred_element_type=jnp.float32)
    return (query_part, key_part, value_part)


def sweep_forward(state, pairs, first_pos, context, block):
    query_four, query_pos, query_docs, ends, scale = context
    count = pairs.shape[0] // block
    split = pairs.reshape((count, block) + pairs.shape[1:])

    def visit(carry, item):
        number, piece = item
        key_first = first_pos + number * block
        key_pos = key_first + jnp.arange(block, dtype=jnp.int32)

        def work(carry_in):
            allowed = block_mask(ends, query_pos, query_docs, key_pos)
            return forward_block(carry_in, query_four, piece[:, 0], piece[:, 1], allowed, scale)

        def unchanged(carry_in):
            return carry_in

        return (
            lax.cond(needed(ends, query_pos, query_docs, key_first, block), work, unchanged, carry),
            None,
        )

    state, _ = lax.scan(visit, state, (jnp.arange(count, dtype=jnp.int32), split))
    return state


def sweep_backward(query_acc, pairs, first_pos, back, block):
    query_pos = back[4]
    query_docs = back[5]
    ends = back[6]
    count = pairs.shape[0] // block
    split = pairs.reshape((count, block) + pairs.shape[1:])

    def visit(carry, item):
        number, piece = item
        key_first = first_pos + number * block
        key_pos = key_first + jnp.arange(block, dtype=jnp.int32)

        def work(carry_in):
            allowed = block_mask(ends, query_pos, query_docs, key_pos)
            query_part, key_part, value_part = backward_block(
                back, piece[:, 0], piece[:, 1], allowed
            )
            return (carry_in + query_part, jnp.stack([key_part, value_part], axis=1))

        def unchanged(carry_in):
            return (carry_in, jnp.zeros(piece.shape, jnp.float32))

        return lax.cond(
            needed(ends, query_pos, query_docs, key_first, block), work, unchanged, carry
        )

    query_acc, partial_grads = lax.scan(
        visit, query_acc, (jnp.arange(count, dtype=jnp.int32), split)
    )
    return (query_acc, partial_grads.reshape(pairs.shape))


def shards(query_rows, key_rows, value_rows, grad_out, lengths):
    tok = query_rows.shape[0]
    kv_heads = key_rows.shape[1] // HD
    q_heads = query_rows.shape[1] // HD
    group = q_heads // kv_heads
    scale = 1.0 / math.sqrt(HD)
    devices = lax.axis_size("seq")
    index = lax.axis_index("seq")
    reach = devices // 2 + 1
    every = lax.all_gather(lengths, "seq", axis=0, tiled=True)
    ends = jnp.cumsum(every)
    query_pos = index * tok + jnp.arange(tok, dtype=jnp.int32)
    query_docs = doc_index(ends, query_pos)
    query_four = query_rows.reshape(tok, kv_heads, group, HD)
    grad_four = grad_out.reshape(tok, kv_heads, group, HD)
    own_pairs = jnp.stack(
        [key_rows.reshape(tok, kv_heads, HD), value_rows.reshape(tok, kv_heads, HD)], axis=1
    )
    context = (query_four, query_pos, query_docs, ends, scale)
    start_state = (
        jnp.full((tok, kv_heads, group), NEGATIVE, jnp.float32),
        jnp.zeros((tok, kv_heads, group), jnp.float32),
        jnp.zeros((tok, kv_heads, group, HD), jnp.float32),
    )
    pairs = own_pairs
    plan = []
    held = 1
    while held < reach + 1:
        extra = min(held, reach + 1 - held)
        arrived = from_behind(pairs[pairs.shape[0] - extra * tok :], "seq", held)
        pairs = jnp.concatenate([arrived, pairs], axis=0)
        plan.append((held, extra))
        held = held + extra
    block = tok * math.gcd(reach + 1, max(1, 512 // tok))
    first_pos = (index - reach) * tok
    state = sweep_forward(start_state, pairs, first_pos, context, block)
    rowmax, rowsum, accum = state
    attended = (accum / rowsum[..., None]).astype(jnp.bfloat16)
    lse = rowmax + jnp.log(rowsum)
    delta = jnp.sum(grad_four.astype(jnp.float32) * attended.astype(jnp.float32), axis=-1)
    back = (query_four, grad_four, lse, delta, query_pos, query_docs, ends, scale)
    zero_query = jnp.zeros((tok, kv_heads, group, HD), jnp.float32)
    query_acc, grads = sweep_backward(zero_query, pairs, first_pos, back, block)
    for held, extra in reversed(plan):
        returned = from_behind(for_sending(grads[: extra * tok]), "seq", -held)
        grads = grads[extra * tok :]
        keep_rows = grads.shape[0] - extra * tok
        grads = jnp.concatenate([grads[:keep_rows], grads[keep_rows:] + returned], axis=0)
    attended_out = attended.reshape(tok, q_heads * HD)
    query_out = (scale * query_acc).astype(jnp.bfloat16).reshape(tok, q_heads * HD)
    key_out = (scale * grads[:, 0]).astype(jnp.bfloat16).reshape(tok, kv_heads * HD)
    value_out = grads[:, 1].astype(jnp.bfloat16).reshape(tok, kv_heads * HD)
    return (attended_out, query_out, key_out, value_out)


def solution(mesh):
    return jax.shard_map(
        shards,
        mesh=mesh,
        in_specs=(
            P(("groups", "seq"), "head"),
            P(("groups", "seq"), "head"),
            P(("groups", "seq"), "head"),
            P(("groups", "seq"), "head"),
            P(("groups", "seq")),
        ),
        out_specs=(
            P(("groups", "seq"), "head"),
            P(("groups", "seq"), "head"),
            P(("groups", "seq"), "head"),
            P(("groups", "seq"), "head"),
        ),
        check_vma=False,
    )
```

profile of v0, /device:TPU:8, one launch (start us, length us, event | category | flops | bytes accessed | tf_op | source)
XLA Modules:
  0.0 104.3 jit_solution(16281358277629973608)
XLA Ops:
  0.6 1.0 copy.52
  1.7 1.0 copy.53
  2.6 3.4 %collective-permute-start = (bf16[128,2,2,128]{0,3,2,1:T(8,128)(2,1)S(1)}, bf16[128,2,2,128]{0,3,2,1:T(8,128)(2,1)S(1)}, u32[]{:S(2)}, u32[]{:S(2)}) collective-permute-start(bf16[128,2,2,128]{0,3,2,1:T(8,128)(2,1)S(1)} %pad_maximum_fusion), channel_id=1, source_target_pairs={{0,2},{2,4},{4,6},{6,8},{8,10},{10,12},{12,14},{1,3},{3,5},{5,7},{... | collective-permute-start | bytes 393224 | tf_op jit(solution)/shard_map/ppermute | solution.py:17
  6.1 4.6 %collective-permute-done = bf16[128,2,2,128]{0,3,2,1:T(8,128)(2,1)S(1)} collective-permute-done((bf16[128,2,2,128]{0,3,2,1:T(8,128)(2,1)S(1)}, bf16[128,2,2,128]{0,3,2,1:T(8,128)(2,1)S(1)}, u32[]{:S(2)}, u32[]{:S(2)}) %collective-permute-start) | collective-permute-done | bytes 131104 | tf_op jit(solution)/shard_map/ppermute | solution.py:17
  10.7 3.5 %collective-permute-start.2 = (bf16[256,2,2,128]{0,3,2,1:T(8,128)(2,1)S(1)}, bf16[256,2,2,128]{0,3,2,1:T(8,128)(2,1)S(1)}, u32[]{:S(2)}, u32[]{:S(2)}) collective-permute-start(bf16[256,2,2,128]{0,3,2,1:T(8,128)(2,1)S(1)} %maximum_maximum_fusion.1), channel_id=1, source_target_pairs={{0,4},{2,6},{4,8},{6,10},{8,12},{10,14},{1,5},{3,7},{5,9},{7,11},{... | collective-permute-start | bytes 786440 | tf_op jit(solution)/shard_map/ppermute | solution.py:17
  14.2 2.3 %collective-permute-start.1 = (bf16[256,2,2,128]{0,3,2,1:T(8,128)(2,1)S(1)}, bf16[256,2,2,128]{0,3,2,1:T(8,128)(2,1)S(1)}, u32[]{:S(2)}, u32[]{:S(2)}) collective-permute-start(bf16[256,2,2,128]{0,3,2,1:T(8,128)(2,1)S(1)} %maximum_maximum_fusion.1), channel_id=1, source_target_pairs={{0,8},{2,10},{4,12},{6,14},{1,9},{3,11},{5,13},{7,15},{16,24},{18,... | collective-permute-start | bytes 786440 | tf_op jit(solution)/shard_map/ppermute | solution.py:17
  16.5 1.2 %dynamic-slice = u32[1]{0:T(128)} dynamic-slice(u32[32]{0:T(128)} %constant.145, u32[]{:T(128)S(6)} %add.131), dynamic_slice_sizes={1} | dynamic-slice | bytes 12
  18.5 0.9 dynamic-update-slice
  19.3 11.0 %all-reduce = s32[32]{0:T(128)S(1)} all-reduce(s32[32]{0:T(128)S(1)} %dynamic-update-slice), channel_id=1, replica_groups=mesh['groups'=2,'seq'=8,'head'=2] {'seq'}, use_global_device_ids=true, to_apply=%add | all-reduce | flops 32 | bytes 256
  30.5 1.3 %copy.59 = bf16[128,2048]{0,1:T(8,128)(2,1)S(1)} copy(bf16[128,2048]{1,0:T(8,128)(2,1)} %param.16) | data formatting | bytes 1048576 | tf_op args[3]
  33.5 16.3 %while.37 = (s32[]{:T(128)}, f32[128,2,8]{0,2,1:T(8,128)S(1)}, f32[128,2,8]{0,2,1:T(8,128)S(1)}, f32[128,2,8,128]{3,0,2,1:T(8,128)S(1)}, s32[3]{0:T(128)S(1)}, /...) while((s32[]{:T(128)}, f32[128,2,8]{0,2,1:T(8,128)S(1)}, ...), condition=%wide.region_9.10_spmd, body=%wide.region_2.9_spmd.sunk | while | flops 275935584 | bytes 9970835 | solution.py:103
  41.1 2.4 %conditional.4 = ((f32[128,2,8]{0,2,1:T(8,128)S(1)}, f32[128,2,8]{0,2,1:T(8,128)S(1)}, f32[128,2,8,128]{3,0,2,1:T(8,128)S(1)})) conditional(s32[]{:T(128)} %convert_element_type.142, (f32[128,2,8]{0,2,1:T(8,128)S(1)}, f32[128,2,8]{0,2,1:T(8,128)S(1)}, f32[128,2,8,128]{3,0,2,1:T(8,128)S(1)}) %tuple.118, (s32[128]{0:T(128)S(1)}, s32[32]{0:T(128)S(1)}, ...), branch_computations={%region_4.4_spmd, %region_5.8_spmd} | conditional | flops 275935488 | bytes 9969320 | solution.py:99
  42.5 1.1 %fusion.3 = f32[128,2,8,128]{3,0,2,1:T(8,128)S(1)} fusion(f32[2,256,128,8]{2,1,3,0:T(8,128)S(1)} %get-tuple-element.788, f32[128,2,8,128]{3,0,2,1:T(8,128)S(1)} %get-tuple-element.589, f32[128,2,8]{0,2,1:T(8,128)S(1)} %max.3, pred[128,256]{0,1:T(8,128)(4,1)S(1)} %and_and_fusion, f32[128,2,8]{0,2,1:T(8,128)S(1)} %get-tuple-element.780, ...), kind=kOutput, calls=%fused_computation.6 | convolution fusion | flops 137363456 | bytes 4374528 | tf_op jit(solution)/shard_map/while/body/eval_jaxpr/cond/branch_1_fun/tagk,kad->tagd/dot_general | solution.py:58
  47.4 2.4 %conditional.4 = ((f32[128,2,8]{0,2,1:T(8,128)S(1)}, f32[128,2,8]{0,2,1:T(8,128)S(1)}, f32[128,2,8,128]{3,0,2,1:T(8,128)S(1)})) conditional(s32[]{:T(128)} %convert_element_type.142, (f32[128,2,8]{0,2,1:T(8,128)S(1)}, f32[128,2,8]{0,2,1:T(8,128)S(1)}, f32[128,2,8,128]{3,0,2,1:T(8,128)S(1)}) %tuple.118, (s32[128]{0:T(128)S(1)}, s32[32]{0:T(128)S(1)}, ...), branch_computations={%region_4.4_spmd, %region_5.8_spmd} | conditional | flops 275935488 | bytes 9969320 | solution.py:99
  48.7 1.1 %fusion.3 = f32[128,2,8,128]{3,0,2,1:T(8,128)S(1)} fusion(f32[2,256,128,8]{2,1,3,0:T(8,128)S(1)} %get-tuple-element.788, f32[128,2,8,128]{3,0,2,1:T(8,128)S(1)} %get-tuple-element.589, f32[128,2,8]{0,2,1:T(8,128)S(1)} %max.3, pred[128,256]{0,1:T(8,128)(4,1)S(1)} %and_and_fusion, f32[128,2,8]{0,2,1:T(8,128)S(1)} %get-tuple-element.780, ...), kind=kOutput, calls=%fused_computation.6 | convolution fusion | flops 137363456 | bytes 4374528 | tf_op jit(solution)/shard_map/while/body/eval_jaxpr/cond/branch_1_fun/tagk,kad->tagd/dot_general | solution.py:58
  49.8 1.3 %copy.58 = f32[128,2,8,128]{0,3,2,1:T(8,128)} copy(f32[128,2,8,128]{3,0,2,1:T(8,128)S(1)} %get-tuple-element.642) | data formatting | bytes 2097152 | tf_op jit(solution)/shard_map/while | solution.py:103
  51.1 2.2 %multiply_reduce_fusion = (f32[128,2,8]{0,2,1:T(8,128)S(1)}, bf16[128,2,8,128]{0,3,2,1:T(8,128)(2,1)}) fusion(bf16[128,2048]{0,1:T(8,128)(2,1)S(1)} %copy.59, f32[128,2,8,128]{0,3,2,1:T(8,128)} %copy.58, f32[128,2,8]{0,2,1:T(8,128)S(1)} %get-tuple-element.643), kind=kLoop, calls=%fused_computation.51 | loop fusion | flops 1570816 | bytes 2113536 | tf_op jit(solution)/shard_map/reduce_sum | solution.py:178
  53.4 20.1 %while.38 = (s32[]{:T(128)}, f32[128,2,8,128]{3,0,2,1:T(8,128)S(1)}, f32[3,256,2,2,128]{4,1,3,2,0:T(8,128)}, s32[3]{0:T(128)S(1)}, s32[]{:T(128)}, /*index=5*/s3...) while((s32[]{:T(128)}, ...), condition=%wide.region_16.17_spmd, body=%wide.region_11.16_spmd.sunk | while | flops 675832192 | bytes 17262212 | solution.py:133
  61.9 3.1 %conditional.5 = (f32[128,2,8,128]{3,0,2,1:T(8,128)S(1)}, f32[1,256,2,2,128]{4,1,3,2,0:T(8,128)S(1)}) conditional(s32[]{:T(128)} %convert_element_type.144, f32[128,2,8,128]{3,0,2,1:T(8,128)S(1)} %get-tuple-element.1022, (s32[128]{0:T(128)S(1)}, s32[32]{0:T(128)S(1)}, s32[]{:T(128)}, s32[256]{0:T(256)S(1)}, s32[128]{0:T(128)S(1)}, ...), branch_computations={%region_13.13_spmd, %region_14.15_spmd} | conditional | flops 675832064 | bytes 16211608 | solution.py:129
  65.0 0.9 constant_dynamic-update-slice_fusion.2
  69.6 3.1 %conditional.5 = (f32[128,2,8,128]{3,0,2,1:T(8,128)S(1)}, f32[1,256,2,2,128]{4,1,3,2,0:T(8,128)S(1)}) conditional(s32[]{:T(128)} %convert_element_type.144, f32[128,2,8,128]{3,0,2,1:T(8,128)S(1)} %get-tuple-element.1022, (s32[128]{0:T(128)S(1)}, s32[32]{0:T(128)S(1)}, s32[]{:T(128)}, s32[256]{0:T(256)S(1)}, s32[128]{0:T(128)S(1)}, ...), branch_computations={%region_13.13_spmd, %region_14.15_spmd} | conditional | flops 675832064 | bytes 16211608 | solution.py:129
  72.7 0.9 constant_dynamic-update-slice_fusion.2
  73.5 1.5 %convert.10 = bf16[3,256,2,2,128]{4,1,3,2,0:T(8,128)(2,1)S(1)} convert(f32[3,256,2,2,128]{4,1,3,2,0:T(8,128)} %get-tuple-element.646) | non-fusion elementwise | flops 393216 | bytes 2359296 | tf_op jit(solution)/shard_map/convert.3
  75.1 1.4 %collective-permute-start.3 = (bf16[256,2,2,128]{3,0,2,1:T(8,128)(2,1)S(1)}, bf16[256,2,2,128]{3,0,2,1:T(8,128)(2,1)S(1)}, u32[]{:S(2)}, u32[]{:S(2)}) collective-permute-start(bf16[256,2,2,128]{3,0,2,1:T(8,128)(2,1)S(1)} %get-tuple-element.789), channel_id=1, source_target_pairs={{8,0},{10,2},{12,4},{14,6},{9,1},{11,3},{13,5},{15,7},{24,16},{26,... | collective-permute-start | bytes 786440 | tf_op jit(solution)/shard_map/ppermute | solution.py:17
  76.6 1.9 %collective-permute-start.4 = (bf16[256,2,2,128]{3,0,2,1:T(8,128)(2,1)S(1)}, bf16[256,2,2,128]{3,0,2,1:T(8,128)(2,1)S(1)}, u32[]{:S(2)}, u32[]{:S(2)}) collective-permute-start(bf16[256,2,2,128]{3,0,2,1:T(8,128)(2,1)S(1)} %get-tuple-element.790), channel_id=1, source_target_pairs={{4,0},{6,2},{8,4},{10,6},{12,8},{14,10},{5,1},{7,3},{9,5},{11,7},{... | collective-permute-start | bytes 786440 | tf_op jit(solution)/shard_map/ppermute | solution.py:17
  78.5 8.3 %collective-permute-done.3 = bf16[256,2,2,128]{3,0,2,1:T(8,128)(2,1)S(1)} collective-permute-done((bf16[256,2,2,128]{3,0,2,1:T(8,128)(2,1)S(1)}, bf16[256,2,2,128]{3,0,2,1:T(8,128)(2,1)S(1)}, u32[]{:S(2)}, u32[]{:S(2)}) %collective-permute-start.3) | collective-permute-done | bytes 262176 | tf_op jit(solution)/shard_map/ppermute | solution.py:17
  86.8 8.6 %collective-permute-done.4 = bf16[256,2,2,128]{3,0,2,1:T(8,128)(2,1)S(1)} collective-permute-done((bf16[256,2,2,128]{3,0,2,1:T(8,128)(2,1)S(1)}, bf16[256,2,2,128]{3,0,2,1:T(8,128)(2,1)S(1)}, u32[]{:S(2)}, u32[]{:S(2)}) %collective-permute-start.4) | collective-permute-done | bytes 262176 | tf_op jit(solution)/shard_map/ppermute | solution.py:17
  95.4 1.1 %fusion.23 = f32[256,2,2,128]{3,0,2,1:T(8,128)S(1)} fusion(bf16[256,2,2,128]{3,0,2,1:T(8,128)(2,1)S(1)} %collective-permute-done.4, bf16[256,2,2,128]{3,0,2,1:T(8,128)(2,1)S(1)} %collective-permute-done.3, f32[3,256,2,2,128]{4,1,3,2,0:T(8,128)} %get-tuple-element.646), kind=kLoop, calls=%fused_computation.56 | loop fusion | flops 524288 | bytes 1572864 | tf_op jit(solution)/shard_map/add | solution.py:186
  96.5 1.9 %collective-permute-start.5 = (bf16[128,2,2,128]{3,0,2,1:T(8,128)(2,1)S(1)}, bf16[128,2,2,128]{3,0,2,1:T(8,128)(2,1)S(1)}, u32[]{:S(2)}, u32[]{:S(2)}) collective-permute-start(bf16[128,2,2,128]{3,0,2,1:T(8,128)(2,1)S(1)} %slice.122), channel_id=1, source_target_pairs={{2,0},{4,2},{6,4},{8,6},{10,8},{12,10},{14,12},{3,1},{5,3},{7,5},{... | collective-permute-start | bytes 393224 | tf_op jit(solution)/shard_map/ppermute | solution.py:17
  98.6 1.0 copy.66
  100.0 0.9 copy.81
  100.9 2.5 %collective-permute-done.5 = bf16[128,2,2,128]{3,0,2,1:T(8,128)(2,1)S(1)} collective-permute-done((bf16[128,2,2,128]{3,0,2,1:T(8,128)(2,1)S(1)}, bf16[128,2,2,128]{3,0,2,1:T(8,128)(2,1)S(1)}, u32[]{:S(2)}, u32[]{:S(2)}) %collective-permute-start.5) | collective-permute-done | bytes 131104 | tf_op jit(solution)/shard_map/ppermute | solution.py:17
  (104 shorter events, 24.0 us)
Async XLA Ops:
  0.6 31.5 %copy-start.1 = (bf16[128,2048]{1,0:T(8,128)(2,1)S(1)}, bf16[128,2048]{1,0:T(8,128)(2,1)}, u32[]{:S(2)}) copy-start(bf16[128,2048]{1,0:T(8,128)(2,1)} %param.13) | copy-start | bytes 1572868
  2.6 8.0 %collective-permute-start = (bf16[128,2,2,128]{0,3,2,1:T(8,128)(2,1)S(1)}, bf16[128,2,2,128]{0,3,2,1:T(8,128)(2,1)S(1)}, u32[]{:S(2)}, u32[]{:S(2)}) collective-permute-start(bf16[128,2,2,128]{0,3,2,1:T(8,128)(2,1)S(1)} %pad_maximum_fusion), channel_id=1, source_target_pairs={{0,2},{2,4},{4,6},{6,8},{8,10},{10,12},{12,14},{1,3},{3,5},{5,7},{... | collective-permute-start | bytes 393224 | tf_op jit(solution)/shard_map/ppermute | solution.py:17
  10.7 22.1 %collective-permute-start.2 = (bf16[256,2,2,128]{0,3,2,1:T(8,128)(2,1)S(1)}, bf16[256,2,2,128]{0,3,2,1:T(8,128)(2,1)S(1)}, u32[]{:S(2)}, u32[]{:S(2)}) collective-permute-start(bf16[256,2,2,128]{0,3,2,1:T(8,128)(2,1)S(1)} %maximum_maximum_fusion.1), channel_id=1, source_target_pairs={{0,4},{2,6},{4,8},{6,10},{8,12},{10,14},{1,5},{3,7},{5,9},{7,11},{... | collective-permute-start | bytes 786440 | tf_op jit(solution)/shard_map/ppermute | solution.py:17
  14.2 18.6 %collective-permute-start.1 = (bf16[256,2,2,128]{0,3,2,1:T(8,128)(2,1)S(1)}, bf16[256,2,2,128]{0,3,2,1:T(8,128)(2,1)S(1)}, u32[]{:S(2)}, u32[]{:S(2)}) collective-permute-start(bf16[256,2,2,128]{0,3,2,1:T(8,128)(2,1)S(1)} %maximum_maximum_fusion.1), channel_id=1, source_target_pairs={{0,8},{2,10},{4,12},{6,14},{1,9},{3,11},{5,13},{7,15},{16,24},{18,... | collective-permute-start | bytes 786440 | tf_op jit(solution)/shard_map/ppermute | solution.py:17
  75.1 23.5 %copy-start = (bf16[128,2,8,128]{0,3,2,1:T(8,128)(2,1)S(1)}, bf16[128,2,8,128]{0,3,2,1:T(8,128)(2,1)}, u32[]{:S(2)}) copy-start(bf16[128,2,8,128]{0,3,2,1:T(8,128)(2,1)} %get-tuple-element.786) | copy-start | bytes 1572868
  75.1 11.6 %collective-permute-start.3 = (bf16[256,2,2,128]{3,0,2,1:T(8,128)(2,1)S(1)}, bf16[256,2,2,128]{3,0,2,1:T(8,128)(2,1)S(1)}, u32[]{:S(2)}, u32[]{:S(2)}) collective-permute-start(bf16[256,2,2,128]{3,0,2,1:T(8,128)(2,1)S(1)} %get-tuple-element.789), channel_id=1, source_target_pairs={{8,0},{10,2},{12,4},{14,6},{9,1},{11,3},{13,5},{15,7},{24,16},{26,... | collective-permute-start | bytes 786440 | tf_op jit(solution)/shard_map/ppermute | solution.py:17
  76.6 18.8 %collective-permute-start.4 = (bf16[256,2,2,128]{3,0,2,1:T(8,128)(2,1)S(1)}, bf16[256,2,2,128]{3,0,2,1:T(8,128)(2,1)S(1)}, u32[]{:S(2)}, u32[]{:S(2)}) collective-permute-start(bf16[256,2,2,128]{3,0,2,1:T(8,128)(2,1)S(1)} %get-tuple-element.790), channel_id=1, source_target_pairs={{4,0},{6,2},{8,4},{10,6},{12,8},{14,10},{5,1},{7,3},{9,5},{11,7},{... | collective-permute-start | bytes 786440 | tf_op jit(solution)/shard_map/ppermute | solution.py:17
  96.5 6.9 %collective-permute-start.5 = (bf16[128,2,2,128]{3,0,2,1:T(8,128)(2,1)S(1)}, bf16[128,2,2,128]{3,0,2,1:T(8,128)(2,1)S(1)}, u32[]{:S(2)}, u32[]{:S(2)}) collective-permute-start(bf16[128,2,2,128]{3,0,2,1:T(8,128)(2,1)S(1)} %slice.122), channel_id=1, source_target_pairs={{2,0},{4,2},{6,4},{8,6},{10,8},{12,10},{14,12},{3,1},{5,3},{7,5},{... | collective-permute-start | bytes 393224 | tf_op jit(solution)/shard_map/ppermute | solution.py:17
where the time goes:
time: 105 us; the launch traced here: 104 us
  waiting for transfers between devices  24 us (23%)
  local copies, waits for them, and re-layouts  21.4 us (20%)
  starting transfers between devices  14.5 us (14%)
  loops' own time  12 us (11%)
  other arithmetic  11.5 us (11%)
  blocking collectives  11 us (10%)
  matrix products  8.35 us (8%)
  between operations  1.61 us (2%)
    ppermute x6, waiting for transfers between devices, from_behind(): lax.ppermute(value, axis, [(source, source + steps) for source in range(l...  24 us
    ppermute x6, starting transfers between devices, from_behind(): lax.ppermute(value, axis, [(source, source + steps) for source in range(l...  14.5 us
    unnamed x1, blocking collectives  11 us
    unnamed x13, local copies, waits for them, and re-layouts  7.6 us
    another operation x1, loops' own time, sweep_forward(): lax.scan(visit, state, (jnp.arange(count, dtype=jnp.int32), split))  5.81 us
    another operation x1, loops' own time, sweep_backward(): lax.scan(visit, query_acc, (jnp.arange(count, dtype=jnp.int32), split))  5.78 us
    reduce_sum x6, other arithmetic, needed(): last_doc = jnp.sum((ends <= key_last).astype(jnp.int32))  3.93 us
    slice x6, local copies, waits for them, and re-layouts, needed(): query_pos[-1]  3.65 us
  transfers between devices with their start and end apart: 6, of which 4 were waited for; matrix products, arithmetic and copies ran while one was open for 7% of the time, Pallas kernels for 0%

commit v1 on v0

v1 whole, which is shorter than its diff:
```python
import functools
import math

import jax
import jax.numpy as jnp
from jax import lax
from jax.experimental import pallas as pl
from jax.experimental.pallas import tpu as pltpu
from jax.sharding import PartitionSpec as P

HD = 128
NEGATIVE = -1e30
MESH = pl.DeviceIdType.MESH


def dot_nt(a, b):
    return lax.dot_general(a, b, (((1,), (1,)), ((), ())), preferred_element_type=jnp.float32)


def dot_nn(a, b):
    return lax.dot_general(a, b, (((1,), (0,)), ((), ())), preferred_element_type=jnp.float32)


def kernel(
    devices,
    q_hbm,
    k_hbm,
    v_hbm,
    g_hbm,
    len_ref,
    att_hbm,
    gq_hbm,
    gk_ref,
    gv_ref,
    qs,
    gs,
    kbuf,
    vbuf,
    sbuf,
    dbuf,
    oacc,
    qacc,
    ostage,
    qstage,
    gsend,
    grecv,
    gown,
    lens,
    start_ref,
    rowmax,
    rowsum,
    delta,
    load_sem,
    kv_sem,
    store_sem,
    k_send,
    k_recv,
    v_send,
    v_recv,
    g_send,
    g_recv,
    l_send,
    l_recv,
):
    heads, rows, _ = qs.shape
    tok = kbuf.shape[1]
    group = rows // tok
    docs = len_ref.shape[0]
    reach = kbuf.shape[0]
    scale = 1.0 / math.sqrt(HD)
    to_exp2 = scale * math.log2(math.e)

    idx = lax.axis_index("seq")
    in_first = idx < reach
    base = jnp.where(in_first, 0, reach)
    local = idx - base
    after = jnp.where(in_first, reach, devices) - base

    own_k = pltpu.make_async_copy(k_hbm, kbuf.at[local], kv_sem.at[0])
    own_v = pltpu.make_async_copy(v_hbm, vbuf.at[local], kv_sem.at[1])
    own_k.start()
    own_v.start()
    loads = []
    for n, (source, target) in enumerate(((q_hbm, qs), (g_hbm, gs))):
        for a in range(heads):
            for h in range(group):
                column = (a * group + h) * HD
                loads.append(
                    pltpu.make_async_copy(
                        source.at[:, pl.ds(column, HD)],
                        target.at[a, pl.ds(h * tok, tok), :],
                        load_sem.at[n, a, h],
                    )
                )
    for copy in loads:
        copy.start()

    barrier = pltpu.get_barrier_semaphore()

    def greet(step, _):
        other = lax.rem(idx + step, devices)
        pl.semaphore_signal(barrier, inc=1, device_id={"seq": other}, device_id_type=MESH)
        return 0

    lax.fori_loop(1, devices, greet, 0)

    lens[idx] = jnp.zeros(lens.shape[1:], jnp.int32)
    for n in range(docs):
        lens[idx, n : n + 1, :] = jnp.full((1, HD), len_ref[n], jnp.int32)
    rowmax[...] = jnp.full(rowmax.shape, NEGATIVE, jnp.float32)
    rowsum[...] = jnp.zeros(rowsum.shape, jnp.float32)
    delta[...] = jnp.zeros(delta.shape, jnp.float32)
    start_ref[...] = jnp.zeros(start_ref.shape, jnp.int32)
    own_k.wait()
    own_v.wait()
    pl.semaphore_wait(barrier, devices - 1)

    def k_copy(target):
        return pltpu.make_async_remote_copy(
            src_ref=kbuf.at[local],
            dst_ref=kbuf.at[local],
            send_sem=k_send.at[target],
            recv_sem=k_recv.at[local],
            device_id={"seq": base + target},
            device_id_type=MESH,
        )

    def v_copy(target):
        return pltpu.make_async_remote_copy(
            src_ref=vbuf.at[local],
            dst_ref=vbuf.at[local],
            send_sem=v_send.at[target],
            recv_sem=v_recv.at[local],
            device_id={"seq": base + target},
            device_id_type=MESH,
        )

    def l_copy(target):
        return pltpu.make_async_remote_copy(
            src_ref=lens.at[idx],
            dst_ref=lens.at[idx],
            send_sem=l_send.at[target],
            recv_sem=l_recv.at[idx],
            device_id={"seq": target},
            device_id_type=MESH,
        )

    def arrival(buf, sem, slot):
        return pltpu.make_async_remote_copy(
            src_ref=buf.at[slot],
            dst_ref=buf.at[slot],
            send_sem=sem.at[slot],
            recv_sem=sem.at[slot],
            device_id={"seq": idx},
            device_id_type=MESH,
        )

    def start_k(n, _):
        k_copy(after - 1 - n).start()
        return 0

    def start_v(n, _):
        v_copy(after - 1 - n).start()
        return 0

    def start_l(target, _):
        @pl.when(target != idx)
        def _():
            l_copy(target).start()

        return 0

    lax.fori_loop(0, after - 1 - local, start_k, 0)
    lax.fori_loop(reach, devices, start_l, 0)
    lax.fori_loop(0, after - 1 - local, start_v, 0)

    for copy in loads[: heads * group]:
        copy.wait()

    @pl.when(jnp.logical_not(in_first))
    def _():
        position = idx * tok + lax.broadcasted_iota(jnp.int32, (1, tok), 1)

        def one(source, carry):
            @pl.when(source != idx)
            def _():
                arrival(lens, l_recv, source).wait_recv()

            total, first = carry
            for n in range(docs):
                total = total + lens[source, n : n + 1, :]
                first = jnp.where(total <= position, total, first)
            return total, first

        zero = jnp.zeros((1, tok), jnp.int32)
        _, first = lax.fori_loop(0, devices, one, (zero, zero))
        start_ref[0:1, :] = first

    key_index = lax.broadcasted_iota(jnp.int32, (tok, tok), 0)
    query_index = lax.broadcasted_iota(jnp.int32, (tok, tok), 1)

    def scores(j, diagonal):
        allowed = (base + j) * tok + key_index >= start_ref[0:1, :]
        if diagonal:
            allowed = allowed & (key_index <= query_index)
        for a in range(heads):
            keys = kbuf[j, :, a * HD : (a + 1) * HD]
            raw = dot_nt(keys, qs[a])
            for h in range(group):
                cols = slice(h * tok, (h + 1) * tok)
                masked = jnp.where(allowed, raw[:, cols], NEGATIVE)
                sbuf[j, a, :, cols] = masked
                rowmax[a, :, cols] = jnp.maximum(
                    rowmax[a, :, cols], jnp.max(masked, axis=0, keepdims=True)
                )

    scores(local, True)

    def scores_step(n, _):
        j = local - 1 - n
        arrival(kbuf, k_recv, j).wait_recv()
        scores(j, False)
        return 0

    lax.fori_loop(0, local, scores_step, 0)

    for copy in loads[heads * group :]:
        copy.wait()

    def weights(j):
        for a in range(heads):
            values = vbuf[j, :, a * HD : (a + 1) * HD]
            dprob = dot_nt(values, gs[a])
            for h in range(group):
                cols = slice(h * tok, (h + 1) * tok)
                expo = jnp.exp2((sbuf[j, a, :, cols] - rowmax[a, :, cols]) * to_exp2)
                sbuf[j, a, :, cols] = expo
                part = dprob[:, cols]
                dbuf[j, a, :, cols] = part
                rowsum[a, :, cols] += jnp.sum(expo, axis=0, keepdims=True)
                delta[a, :, cols] += jnp.sum(expo * part, axis=0, keepdims=True)

    weights(local)

    def weights_step(n, _):
        j = local - 1 - n
        arrival(vbuf, v_recv, j).wait_recv()
        weights(j)
        return 0

    lax.fori_loop(0, local, weights_step, 0)

    rowsum[...] = 1.0 / rowsum[...]
    delta[...] = delta[...] * rowsum[...]
    oacc[...] = jnp.zeros(oacc.shape, jnp.float32)
    qacc[...] = jnp.zeros(qacc.shape, jnp.float32)

    def gradients(j, store):
        for a in range(heads):
            prob = sbuf[j, a] * rowsum[a]
            prob_low = prob.astype(jnp.bfloat16)
            dscore = (prob * (dbuf[j, a] - delta[a])).astype(jnp.bfloat16)
            cols = slice(a * HD, (a + 1) * HD)
            store(cols, dot_nn(dscore, qs[a]), dot_nn(prob_low, gs[a]))
            oacc[a] += dot_nn(vbuf[j, :, cols].T, prob_low)
            qacc[a] += dot_nn(kbuf[j, :, cols].T, dscore)

    def g_copy(j):
        return pltpu.make_async_remote_copy(
            src_ref=gsend.at[j],
            dst_ref=grecv.at[local],
            send_sem=g_send.at[j],
            recv_sem=g_recv.at[local],
            device_id={"seq": base + j},
            device_id_type=MESH,
        )

    def gradients_step(j, _):
        def store(cols, key_part, value_part):
            gsend[j, 0, :, cols] = key_part.astype(jnp.bfloat16)
            gsend[j, 1, :, cols] = value_part.astype(jnp.bfloat16)

        gradients(j, store)
        g_copy(j).start()
        return 0

    lax.fori_loop(0, local, gradients_step, 0)

    def store_own(cols, key_part, value_part):
        gown[0, :, cols] = key_part
        gown[1, :, cols] = value_part

    gradients(local, store_own)

    stores = []
    for a in range(heads):
        for h in range(group):
            cols = slice(h * tok, (h + 1) * tok)
            ostage[a, cols, :] = oacc[a, :, cols].T.astype(jnp.bfloat16)
            qstage[a, cols, :] = (scale * qacc[a, :, cols]).T.astype(jnp.bfloat16)
            column = (a * group + h) * HD
            for n, (source, target) in enumerate(((ostage, att_hbm), (qstage, gq_hbm))):
                copy = pltpu.make_async_copy(
                    source.at[a, pl.ds(h * tok, tok), :],
                    target.at[:, pl.ds(column, HD)],
                    store_sem.at[n, a, h],
                )
                copy.start()
                stores.append(copy)

    def collect(j, _):
        arrival(grecv, g_recv, j).wait_recv()
        gown[...] += grecv[j].astype(jnp.float32)
        return 0

    lax.fori_loop(local + 1, after, collect, 0)
    gk_ref[...] = (scale * gown[0]).astype(jnp.bfloat16)
    gv_ref[...] = gown[1].astype(jnp.bfloat16)

    for copy in stores:
        copy.wait()

    def end_kv(target, _):
        k_copy(target).wait_send()
        v_copy(target).wait_send()
        return 0

    def end_l(target, _):
        @pl.when(target != idx)
        def _():
            l_copy(target).wait_send()

        return 0

    def end_g(j, _):
        g_copy(j).wait_send()
        return 0

    lax.fori_loop(local + 1, after, end_kv, 0)
    lax.fori_loop(reach, devices, end_l, 0)
    lax.fori_loop(0, local, end_g, 0)


def shards(query_rows, key_rows, value_rows, grad_out, lengths):
    tok, width = query_rows.shape
    heads = key_rows.shape[1] // HD
    group = width // HD // heads
    devices = lax.axis_size("seq")
    reach = devices // 2 + 1
    rows = group * tok
    docs = -(-lengths.shape[0] // 8) * 8
    anywhere = pl.BlockSpec(memory_space=pl.ANY)
    vmem = pl.BlockSpec(memory_space=pltpu.VMEM)
    dma = pltpu.SemaphoreType.DMA
    bf16, f32 = jnp.bfloat16, jnp.float32
    pairs = devices * rows * tok * heads
    return pl.pallas_call(
        functools.partial(kernel, devices),
        out_shape=(
            jax.ShapeDtypeStruct(query_rows.shape, bf16),
            jax.ShapeDtypeStruct(query_rows.shape, bf16),
            jax.ShapeDtypeStruct(key_rows.shape, bf16),
            jax.ShapeDtypeStruct(value_rows.shape, bf16),
        ),
        in_specs=[anywhere] * 4 + [pl.BlockSpec(memory_space=pltpu.SMEM)],
        out_specs=(anywhere, anywhere, vmem, vmem),
        scratch_shapes=[
            pltpu.VMEM((heads, rows, HD), bf16),
            pltpu.VMEM((heads, rows, HD), bf16),
            pltpu.VMEM((reach, tok, heads * HD), bf16),
            pltpu.VMEM((reach, tok, heads * HD), bf16),
            pltpu.VMEM((reach, heads, tok, rows), f32),
            pltpu.VMEM((reach, heads, tok, rows), f32),
            pltpu.VMEM((heads, HD, rows), f32),
            pltpu.VMEM((heads, HD, rows), f32),
            pltpu.VMEM((heads, rows, HD), bf16),
            pltpu.VMEM((heads, rows, HD), bf16),
            pltpu.VMEM((reach, 2, tok, heads * HD), bf16),
            pltpu.VMEM((reach, 2, tok, heads * HD), bf16),
            pltpu.VMEM((2, tok, heads * HD), f32),
            pltpu.VMEM((devices, docs, HD), jnp.int32),
            pltpu.VMEM((8, tok), jnp.int32),
            pltpu.VMEM((heads, 1, rows), f32),
            pltpu.VMEM((heads, 1, rows), f32),
            pltpu.VMEM((heads, 1, rows), f32),
            dma((2, heads, group)),
            dma((2,)),
            dma((2, heads, group)),
            dma((reach,)),
            dma((reach,)),
            dma((reach,)),
            dma((reach,)),
            dma((reach,)),
            dma((reach,)),
            dma((devices,)),
            dma((devices,)),
        ],
        compiler_params=pltpu.CompilerParams(
            collective_id=0, has_side_effects=True, vmem_limit_bytes=56 * 1024 * 1024
        ),
        cost_estimate=pl.CostEstimate(
            flops=6 * pairs * HD, bytes_accessed=8 * tok * width, transcendentals=pairs
        ),
    )(query_rows, key_rows, value_rows, grad_out, lengths)


def solution(mesh):
    split = P(("groups", "seq"), "head")
    return jax.shard_map(
        shards,
        mesh=mesh,
        in_specs=(split, split, split, split, P(("groups", "seq"))),
        out_specs=(split, split, split, split),
        check_vma=False,
    )
```

time: 105 us -> 33.9 us (0.32)
  the two profiles are of different devices: /device:TPU:8 before, /device:TPU:4 now
where the time goes in v1:
time: 33.9 us; the launch traced here: 33.6 us
  Pallas kernels  28.6 us (84%)
  local copies, waits for them, and re-layouts  4.3 us (13%)
  between operations  0.65 us (2%)
    pallas_call x1, Pallas kernels, shards(): pl.pallas_call(functools.partial(kernel, devices), out_shape=(jax.ShapeDt...  28.6 us
    unnamed x10, local copies, waits for them, and re-layouts  4.3 us

profile of v1, /device:TPU:4, one launch (start us, length us, event | category | flops | bytes accessed | tf_op | source)
XLA Modules:
  0.0 33.6 jit_solution(10007721634733064502)
XLA Ops:
  0.6 28.6 %shard_map.84 = (bf16[128,2048]{1,0:T(8,128)(2,1)}, bf16[128,2048]{1,0:T(8,128)(2,1)}, bf16[128,256]{1,0:T(8,128)(2,1)}, bf16[128,256]{1,0:T(8,128)(2,1)}) custom-call(bf16[128,2048]{1,0:T(8,128)(2,1)} %q_hbm.1, bf16[128,256]{1,0:T(8,128)(2,1)} %k_hbm.1, bf16[128,256]{1,0:T(8,128)(2,1)} %v_hbm.1, bf16[128,2048]{1,0:T(8,128)(2,1)} %g_hbm.1, s32[4]{0:T(128)} %len_ref.1), custom_call_target="tpu_custom_call" | custom-call | flops 1610612736 | bytes 2097152 | tf_op jit(solution)/shard_map/pallas_call | solution.py:357
  29.3 0.0 copy-start
  29.3 1.9 %copy.13 = bf16[128,2048]{1,0:T(8,128)(2,1)} copy(bf16[128,2048]{1,0:T(8,128)(2,1)} %get-tuple-element.8) | data formatting | bytes 1048576
  31.2 0.0 copy-done
  31.2 0.0 copy-start.2
  31.2 0.8 %copy.14 = bf16[128,2048]{1,0:T(8,128)(2,1)} copy(bf16[128,2048]{1,0:T(8,128)(2,1)S(1)} %copy-done) | data formatting | bytes 1048576
  32.0 0.1 copy-done.2
  32.1 0.0 copy-start.1
  32.1 0.6 %copy.15 = bf16[128,256]{1,0:T(8,128)(2,1)} copy(bf16[128,256]{1,0:T(8,128)(2,1)S(1)} %copy-done.2) | data formatting | bytes 131072
  32.7 0.2 copy-done.1
  33.0 0.6 %copy.16 = bf16[128,256]{1,0:T(8,128)(2,1)} copy(bf16[128,256]{1,0:T(8,128)(2,1)S(1)} %copy-done.1) | data formatting | bytes 131072
Async XLA Ops:
  29.3 2.0 %copy-start = (bf16[128,2048]{1,0:T(8,128)(2,1)S(1)}, bf16[128,2048]{1,0:T(8,128)(2,1)}, u32[]{:S(2)}) copy-start(bf16[128,2048]{1,0:T(8,128)(2,1)} %get-tuple-element.9) | copy-start | bytes 1572868
  31.2 0.9 %copy-start.2 = (bf16[128,256]{1,0:T(8,128)(2,1)S(1)}, bf16[128,256]{1,0:T(8,128)(2,1)}, u32[]{:S(2)}) copy-start(bf16[128,256]{1,0:T(8,128)(2,1)} %get-tuple-element.10) | copy-start | bytes 196612
  32.1 0.9 %copy-start.1 = (bf16[128,256]{1,0:T(8,128)(2,1)S(1)}, bf16[128,256]{1,0:T(8,128)(2,1)}, u32[]{:S(2)}) copy-start(bf16[128,256]{1,0:T(8,128)(2,1)} %get-tuple-element.11) | copy-start | bytes 196612

commit v2 on v1

v2 whole, which is shorter than its diff:
```python
import functools
import math

import jax
import jax.numpy as jnp
from jax import lax
from jax.experimental import pallas as pl
from jax.experimental.pallas import tpu as pltpu
from jax.sharding import PartitionSpec as P

HD = 128
NEGATIVE = -1e30
MESH = pl.DeviceIdType.MESH
UNROLLED = 8


def dot_nt(a, b):
    return lax.dot_general(a, b, (((1,), (1,)), ((), ())), preferred_element_type=jnp.float32)


def dot_nn(a, b):
    return lax.dot_general(a, b, (((1,), (0,)), ((), ())), preferred_element_type=jnp.float32)


def stacked(ref, first, count):
    return jnp.concatenate(
        [ref[:, (first + h) * HD : (first + h + 1) * HD] for h in range(count)], axis=0
    )


def kernel(
    devices,
    q_hbm,
    k_hbm,
    v_hbm,
    g_hbm,
    len_ref,
    att_hbm,
    gq_hbm,
    gk_ref,
    gv_ref,
    qbuf,
    gbuf,
    kv,
    probs,
    dscores,
    ostage,
    qstage,
    gsend,
    grecv,
    gown,
    lens,
    start_ref,
    load_sem,
    kv_sem,
    store_sem,
    kv_send,
    kv_recv,
    g_send,
    g_recv,
    l_send,
    l_recv,
    *loop_refs,
):
    heads, reach, _, tok, _ = kv.shape
    group = qbuf.shape[1] // HD // heads
    docs = len_ref.shape[0]
    scale = 1.0 / math.sqrt(HD)
    to_exp2 = scale * math.log2(math.e)
    wide = 2 if group % 2 == 0 else 1

    idx = lax.axis_index("seq")
    in_first = idx < reach
    base = jnp.where(in_first, 0, reach)
    local = idx - base
    after = jnp.where(in_first, reach, devices) - base

    own = []
    for a in range(heads):
        for n, source in enumerate((k_hbm, v_hbm)):
            own.append(
                pltpu.make_async_copy(
                    source.at[:, pl.ds(a * HD, HD)], kv.at[a, local, n], kv_sem.at[a, n]
                )
            )
    loads = []
    for a in range(heads):
        cols = pl.ds(a * group * HD, group * HD)
        for n, (source, target) in enumerate(((q_hbm, qbuf), (g_hbm, gbuf))):
            loads.append(
                pltpu.make_async_copy(source.at[:, cols], target.at[:, cols], load_sem.at[a, n])
            )
    for copy in own + loads:
        copy.start()

    barrier = pltpu.get_barrier_semaphore()

    def greet(step, _):
        other = lax.rem(idx + step, devices)
        pl.semaphore_signal(barrier, inc=1, device_id={"seq": other}, device_id_type=MESH)
        return 0

    lax.fori_loop(1, devices, greet, 0)

    lens[idx] = jnp.zeros(lens.shape[1:], jnp.int32)
    for n in range(docs):
        lens[idx, n : n + 1, :] = jnp.full((1, HD), len_ref[n], jnp.int32)
    start_ref[...] = jnp.zeros(start_ref.shape, jnp.int32)
    for copy in own:
        copy.wait()
    pl.semaphore_wait(barrier, devices - 1)

    def l_copy(target):
        return pltpu.make_async_remote_copy(
            src_ref=lens.at[idx],
            dst_ref=lens.at[idx],
            send_sem=l_send.at[target],
            recv_sem=l_recv.at[idx],
            device_id={"seq": target},
            device_id_type=MESH,
        )

    def kv_copy(a, target):
        return pltpu.make_async_remote_copy(
            src_ref=kv.at[a, local],
            dst_ref=kv.at[a, local],
            send_sem=kv_send.at[a, target],
            recv_sem=kv_recv.at[a, local],
            device_id={"seq": base + target},
            device_id_type=MESH,
        )

    def g_copy(a, j):
        return pltpu.make_async_remote_copy(
            src_ref=gsend.at[a, j],
            dst_ref=grecv.at[a, local],
            send_sem=g_send.at[a, j],
            recv_sem=g_recv.at[a, local],
            device_id={"seq": base + j},
            device_id_type=MESH,
        )

    def arrival(buf, sem):
        return pltpu.make_async_remote_copy(
            src_ref=buf,
            dst_ref=buf,
            send_sem=sem,
            recv_sem=sem,
            device_id={"seq": idx},
            device_id_type=MESH,
        )

    def start_l(target, _):
        @pl.when(target != idx)
        def _():
            l_copy(target).start()

        return 0

    lax.fori_loop(reach, devices, start_l, 0)
    for a in range(heads):

        def start_kv(n, _, a=a):
            kv_copy(a, after - 1 - n).start()
            return 0

        lax.fori_loop(0, after - 1 - local, start_kv, 0)

    @pl.when(jnp.logical_not(in_first))
    def _():
        position = idx * tok + lax.broadcasted_iota(jnp.int32, (1, tok), 1)

        def one(source, carry):
            @pl.when(source != idx)
            def _():
                arrival(lens.at[source], l_recv.at[source]).wait_recv()

            total, first = carry
            for n in range(docs):
                total = total + lens[source, n : n + 1, :]
                first = jnp.where(total <= position, total, first)
            return total, first

        zero = jnp.zeros((1, tok), jnp.int32)
        _, first = lax.fori_loop(0, devices, one, (zero, zero))
        for h in range(wide):
            start_ref[0:1, h * tok : (h + 1) * tok] = first

    def one_count(count):
        size = count * tok
        key_index = lax.broadcasted_iota(jnp.int32, (size, wide * tok), 0)
        query_index = lax.rem(lax.broadcasted_iota(jnp.int32, (tok, wide * tok), 1), tok)
        causal = lax.broadcasted_iota(jnp.int32, (tok, wide * tok), 0) <= query_index
        for a in range(heads):
            for j in range(count - 1):
                arrival(kv.at[a, j], kv_recv.at[a, j]).wait_recv()
            loads[2 * a].wait()
            loads[2 * a + 1].wait()
            keys = kv[a, 0:count, 0].reshape(size, HD)
            values = kv[a, 0:count, 1].reshape(size, HD)
            keys_t = keys.T
            values_t = values.T
            for p in range(group // wide):
                first = a * group + p * wide
                queries = stacked(qbuf, first, wide)
                cotangents = stacked(gbuf, first, wide)
                raw = dot_nt(keys, queries)
                if count <= devices - reach:
                    raw = jnp.where(base * tok + key_index >= start_ref[0:1, :], raw, NEGATIVE)
                last = jnp.where(causal, raw[size - tok :], NEGATIVE)
                raw = jnp.concatenate([raw[: size - tok], last], axis=0) if count > 1 else last
                rowmax = jnp.max(raw, axis=0, keepdims=True)
                expo = jnp.exp2((raw - rowmax) * to_exp2)
                dprob = dot_nt(values, cotangents)
                inverse = 1.0 / jnp.sum(expo, axis=0, keepdims=True)
                delta = jnp.sum(expo * dprob, axis=0, keepdims=True) * inverse
                prob = expo * inverse
                prob_low = prob.astype(jnp.bfloat16)
                dscore = (prob * (dprob - delta)).astype(jnp.bfloat16)
                wide_cols = slice(p * wide * tok, (p + 1) * wide * tok)
                probs[0:size, wide_cols] = prob_low
                dscores[0:size, wide_cols] = dscore
                out = dot_nn(values_t, prob_low)
                grad = scale * dot_nn(keys_t, dscore)
                for h in range(wide):
                    cols = slice((first + h) * HD, (first + h + 1) * HD)
                    part = slice(h * tok, (h + 1) * tok)
                    ostage[:, cols] = out[:, part].T.astype(jnp.bfloat16)
                    qstage[:, cols] = grad[:, part].T.astype(jnp.bfloat16)
            key_part = dot_nn(dscores[0:size, :], stacked(qbuf, a * group, group))
            value_part = dot_nn(probs[0:size, :], stacked(gbuf, a * group, group))
            for j in range(count - 1):
                piece = slice(j * tok, (j + 1) * tok)
                gsend[a, j, 0] = key_part[piece].astype(jnp.bfloat16)
                gsend[a, j, 1] = value_part[piece].astype(jnp.bfloat16)
                g_copy(a, j).start()
            gown[a, 0] = key_part[size - tok :]
            gown[a, 1] = value_part[size - tok :]

    def any_count(sbuf, dbuf, oacc, qacc, rowmax, rowsum, delta):
        key_index = lax.broadcasted_iota(jnp.int32, (tok, tok), 0)
        query_index = lax.broadcasted_iota(jnp.int32, (tok, tok), 1)
        for a in range(heads):
            loads[2 * a].wait()
            loads[2 * a + 1].wait()
            queries = stacked(qbuf, a * group, group)
            cotangents = stacked(gbuf, a * group, group)
            rowmax[...] = jnp.full(rowmax.shape, NEGATIVE, jnp.float32)
            rowsum[...] = jnp.zeros(rowsum.shape, jnp.float32)
            delta[...] = jnp.zeros(delta.shape, jnp.float32)
            oacc[...] = jnp.zeros(oacc.shape, jnp.float32)
            qacc[...] = jnp.zeros(qacc.shape, jnp.float32)

            def first_pass(j, diagonal):
                allowed = (base + j) * tok + key_index >= start_ref[0:1, 0:tok]
                if diagonal:
                    allowed = allowed & (key_index <= query_index)
                raw = dot_nt(kv[a, j, 0], queries)
                for h in range(group):
                    cols = slice(h * tok, (h + 1) * tok)
                    masked = jnp.where(allowed, raw[:, cols], NEGATIVE)
                    sbuf[j, :, cols] = masked
                    rowmax[:, cols] = jnp.maximum(
                        rowmax[:, cols], jnp.max(masked, axis=0, keepdims=True)
                    )

            def first_step(j, _):
                arrival(kv.at[a, j], kv_recv.at[a, j]).wait_recv()
                first_pass(j, False)
                return 0

            first_pass(local, True)
            lax.fori_loop(0, local, first_step, 0)

            def second_step(j, _):
                dprob = dot_nt(kv[a, j, 1], cotangents)
                expo = jnp.exp2((sbuf[j] - rowmax[...]) * to_exp2)
                sbuf[j] = expo
                dbuf[j] = dprob
                rowsum[...] += jnp.sum(expo, axis=0, keepdims=True)
                delta[...] += jnp.sum(expo * dprob, axis=0, keepdims=True)
                return 0

            lax.fori_loop(0, local + 1, second_step, 0)
            rowsum[...] = 1.0 / rowsum[...]
            delta[...] = delta[...] * rowsum[...]

            def third_pass(j):
                prob = sbuf[j] * rowsum[...]
                prob_low = prob.astype(jnp.bfloat16)
                dscore = (prob * (dbuf[j] - delta[...])).astype(jnp.bfloat16)
                oacc[...] += dot_nn(kv[a, j, 1].T, prob_low)
                qacc[...] += dot_nn(kv[a, j, 0].T, dscore)
                return dot_nn(dscore, queries), dot_nn(prob_low, cotangents)

            def third_step(j, _):
                key_part, value_part = third_pass(j)
                gsend[a, j, 0] = key_part.astype(jnp.bfloat16)
                gsend[a, j, 1] = value_part.astype(jnp.bfloat16)
                g_copy(a, j).start()
                return 0

            lax.fori_loop(0, local, third_step, 0)
            gown[a, 0], gown[a, 1] = third_pass(local)
            for h in range(group):
                cols = slice((a * group + h) * HD, (a * group + h + 1) * HD)
                part = slice(h * tok, (h + 1) * tok)
                ostage[:, cols] = oacc[:, part].T.astype(jnp.bfloat16)
                qstage[:, cols] = (scale * qacc[:, part]).T.astype(jnp.bfloat16)

    if loop_refs:
        any_count(*loop_refs)
    else:
        for count in range(1, reach + 1):
            pl.when(local + 1 == count)(functools.partial(one_count, count))

    stores = [
        pltpu.make_async_copy(ostage, att_hbm, store_sem.at[0]),
        pltpu.make_async_copy(qstage, gq_hbm, store_sem.at[1]),
    ]
    for copy in stores:
        copy.start()

    for a in range(heads):

        def collect(j, _, a=a):
            arrival(grecv.at[a, j], g_recv.at[a, j]).wait_recv()
            gown[a] += grecv[a, j].astype(jnp.float32)
            return 0

        lax.fori_loop(local + 1, after, collect, 0)
        cols = slice(a * HD, (a + 1) * HD)
        gk_ref[:, cols] = (scale * gown[a, 0]).astype(jnp.bfloat16)
        gv_ref[:, cols] = gown[a, 1].astype(jnp.bfloat16)

    for copy in stores:
        copy.wait()

    def end_l(target, _):
        @pl.when(target != idx)
        def _():
            l_copy(target).wait_send()

        return 0

    lax.fori_loop(reach, devices, end_l, 0)
    for a in range(heads):

        def end_kv(target, _, a=a):
            kv_copy(a, target).wait_send()
            return 0

        def end_g(j, _, a=a):
            g_copy(a, j).wait_send()
            return 0

        lax.fori_loop(local + 1, after, end_kv, 0)
        lax.fori_loop(0, local, end_g, 0)


def hand_on(*refs):
    count = len(refs) // 2
    sems = refs[-1]
    copies = [
        pltpu.make_async_copy(refs[n], refs[count + n], sems.at[n]) for n in range(count)
    ]
    for copy in copies:
        copy.start()
    for copy in copies:
        copy.wait()


def shards(query_rows, key_rows, value_rows, grad_out, lengths):
    tok, width = query_rows.shape
    heads = key_rows.shape[1] // HD
    group = width // HD // heads
    devices = lax.axis_size("seq")
    reach = devices // 2 + 1
    rows = group * tok
    docs = -(-lengths.shape[0] // 8) * 8
    wide = 2 if group % 2 == 0 else 1
    unrolled = reach <= UNROLLED
    held = reach * tok if unrolled else 16
    anywhere = pl.BlockSpec(memory_space=pl.ANY)
    vmem = pl.BlockSpec(memory_space=pltpu.VMEM)
    dma = pltpu.SemaphoreType.DMA
    bf16, f32 = jnp.bfloat16, jnp.float32
    loop_scratch = [
        pltpu.VMEM((reach, tok, rows), f32),
        pltpu.VMEM((reach, tok, rows), f32),
        pltpu.VMEM((HD, rows), f32),
        pltpu.VMEM((HD, rows), f32),
        pltpu.VMEM((1, rows), f32),
        pltpu.VMEM((1, rows), f32),
        pltpu.VMEM((1, rows), f32),
    ]
    pairs = reach * rows * tok * heads
    shapes = (
        jax.ShapeDtypeStruct(query_rows.shape, bf16),
        jax.ShapeDtypeStruct(query_rows.shape, bf16),
        jax.ShapeDtypeStruct(key_rows.shape, bf16),
        jax.ShapeDtypeStruct(value_rows.shape, bf16),
    )
    results = pl.pallas_call(
        functools.partial(kernel, devices),
        out_shape=shapes,
        in_specs=[anywhere] * 4 + [pl.BlockSpec(memory_space=pltpu.SMEM)],
        out_specs=(anywhere, anywhere, vmem, vmem),
        scratch_shapes=[
            pltpu.VMEM((tok, width), bf16),
            pltpu.VMEM((tok, width), bf16),
            pltpu.VMEM((heads, reach, 2, tok, HD), bf16),
            pltpu.VMEM((held, rows), bf16),
            pltpu.VMEM((held, rows), bf16),
            pltpu.VMEM((tok, width), bf16),
            pltpu.VMEM((tok, width), bf16),
            pltpu.VMEM((heads, reach, 2, tok, HD), bf16),
            pltpu.VMEM((heads, reach, 2, tok, HD), bf16),
            pltpu.VMEM((heads, 2, tok, HD), f32),
            pltpu.VMEM((devices, docs, HD), jnp.int32),
            pltpu.VMEM((1, wide * tok), jnp.int32),
            dma((heads, 2)),
            dma((heads, 2)),
            dma((2,)),
            dma((heads, reach)),
            dma((heads, reach)),
            dma((heads, reach)),
            dma((heads, reach)),
            dma((devices,)),
            dma((devices,)),
        ]
        + ([] if unrolled else loop_scratch),
        compiler_params=pltpu.CompilerParams(
            collective_id=0, has_side_effects=True, vmem_limit_bytes=56 * 1024 * 1024
        ),
        cost_estimate=pl.CostEstimate(
            flops=12 * pairs * HD, bytes_accessed=8 * tok * width, transcendentals=pairs
        ),
    )(query_rows, key_rows, value_rows, grad_out, lengths)
    return pl.pallas_call(
        hand_on,
        out_shape=shapes,
        in_specs=[anywhere] * 4,
        out_specs=(anywhere,) * 4,
        scratch_shapes=[dma((4,))],
        cost_estimate=pl.CostEstimate(
            flops=0, bytes_accessed=8 * tok * width, transcendentals=0
        ),
    )(*results)


def solution(mesh):
    split = P(("groups", "seq"), "head")
    return jax.shard_map(
        shards,
        mesh=mesh,
        in_specs=(split, split, split, split, P(("groups", "seq"))),
        out_specs=(split, split, split, split),
        check_vma=False,
    )
```

time: 33.9 us -> 65.2 us (1.92)
  the two profiles are of different devices: /device:TPU:4 before, /device:TPU:0 now
where the time goes in v2:
time: 65.2 us; the launch traced here: 65 us
  Pallas kernels  64.2 us (98%)
  between operations  0.8 us (1%)
    pallas_call x1, Pallas kernels, shards(): pl.pallas_call(hand_on, out_shape=shapes, in_specs=[anywhere] * 4, out_sp...  36.9 us
    pallas_call x1, Pallas kernels, shards(): pl.pallas_call(functools.partial(kernel, devices), out_shape=shapes, in_s...  27.4 us

profile of v2, /device:TPU:0, one launch (start us, length us, event | category | flops | bytes accessed | tf_op | source)
XLA Modules:
  0.0 65.0 jit_solution(10451122091765562434)
XLA Ops:
  0.6 27.4 %shard_map.84 = (bf16[128,2048]{1,0:T(8,128)(2,1)}, bf16[128,2048]{1,0:T(8,128)(2,1)}, bf16[128,256]{1,0:T(8,128)(2,1)}, bf16[128,256]{1,0:T(8,128)(2,1)}) custom-call(bf16[128,2048]{1,0:T(8,128)(2,1)} %q_hbm.1, bf16[128,256]{1,0:T(8,128)(2,1)} %k_hbm.1, bf16[128,256]{1,0:T(8,128)(2,1)} %v_hbm.1, bf16[128,2048]{1,0:T(8,128)(2,1)} %g_hbm.1, s32[4]{0:T(128)} %len_ref.1), custom_call_target="tpu_custom_call" | custom-call | flops 2013265920 | bytes 2097152 | tf_op jit(solution)/shard_map/pallas_call | solution.py:404
  28.0 36.9 %shard_map.85 = (bf16[128,2048]{1,0:T(8,128)(2,1)}, bf16[128,2048]{1,0:T(8,128)(2,1)}, bf16[128,256]{1,0:T(8,128)(2,1)}, bf16[128,256]{1,0:T(8,128)(2,1)}) custom-call(bf16[128,2048]{1,0:T(8,128)(2,1)} %get-tuple-element.8.refs_0_, bf16[128,2048]{1,0:T(8,128)(2,1)} %get-tuple-element.9.refs_1_, bf16[128,256]{1,0:T(8,128)(2,1)} %get-tuple-element.10.refs_2_, ...), custom_call_target="tpu_custom_call" | custom-call | bytes 2097152 | tf_op jit(solution)/shard_map/pallas_call | solution.py:440

commit v3 on v2

--- a/solution.py
+++ b/solution.py
@@ -60,9 +60,19 @@
     g_recv,
     l_send,
     l_recv,
+    kv_relay,
+    g_relay,
+    kr_send,
+    kr_recv,
+    gr_send,
+    gr_recv,
+    kf_send,
+    gf_send,
     *loop_refs,
 ):
     heads, reach, _, tok, _ = kv.shape
+    relaying = not loop_refs and reach < devices
+    relayed = [j for j in range(reach - 1) if (reach - 1 - j) % 2] if relaying else []
     group = qbuf.shape[1] // HD // heads
     docs = len_ref.shape[0]
     scale = 1.0 / math.sqrt(HD)
@@ -140,6 +150,52 @@
             device_id_type=MESH,
         )
 
+    def kv_to_relay(a, j):
+        return pltpu.make_async_remote_copy(
+            src_ref=kv.at[a, j],
+            dst_ref=kv_relay.at[a, j],
+            send_sem=kr_send.at[a],
+            recv_sem=kr_recv.at[a, j],
+            device_id={"seq": reach},
+            device_id_type=MESH,
+        )
+
+    def kv_forward(a, j):
+        return pltpu.make_async_remote_copy(
+            src_ref=kv_relay.at[a, j],
+            dst_ref=kv.at[a, j],
+            send_sem=kf_send.at[a, j],
+            recv_sem=kv_recv.at[a, j],
+            device_id={"seq": reach - 1},
+            device_id_type=MESH,
+        )
+
+    def g_to_relay(a, j):
+        return pltpu.make_async_remote_copy(
+            src_ref=gsend.at[a, j],
+            dst_ref=g_relay.at[a, j],
+            send_sem=gr_send.at[a, j],
+            recv_sem=gr_recv.at[a, j],
+            device_id={"seq": reach},
+            device_id_type=MESH,
+        )
+
+    def g_forward(a, j):
+        return pltpu.make_async_remote_copy(
+            src_ref=g_relay.at[a, j],
+            dst_ref=grecv.at[a, reach - 1],
+            send_sem=gf_send.at[a, j],
+            recv_sem=g_recv.at[a, reach - 1],
+            device_id={"seq": j},
+            device_id_type=MESH,
+        )
+
+    def is_relayed(j):
+        found = idx < 0
+        for other in relayed:
+            found = jnp.logical_or(found, j == other)
+        return found
+
     def arrival(buf, sem):
         return pltpu.make_async_remote_copy(
             src_ref=buf,
@@ -157,14 +213,26 @@
 
         return 0
 
+    skip = jnp.where(in_first & is_relayed(idx), 1, 0)
     lax.fori_loop(reach, devices, start_l, 0)
     for a in range(heads):
+        for j in relayed:
+            pl.when(idx == j)(kv_to_relay(a, j).start)
 
         def start_kv(n, _, a=a):
             kv_copy(a, after - 1 - n).start()
             return 0
 
-        lax.fori_loop(0, after - 1 - local, start_kv, 0)
+        lax.fori_loop(skip, after - 1 - local, start_kv, 0)
+
+    if relaying:
+
+        @pl.when(idx == reach)
+        def _():
+            for a in range(heads):
+                for j in relayed:
+                    kv_to_relay(a, j).wait_recv()
+                    kv_forward(a, j).start()
 
     @pl.when(jnp.logical_not(in_first))
     def _():
@@ -233,7 +301,7 @@
                 piece = slice(j * tok, (j + 1) * tok)
                 gsend[a, j, 0] = key_part[piece].astype(jnp.bfloat16)
                 gsend[a, j, 1] = value_part[piece].astype(jnp.bfloat16)
-                g_copy(a, j).start()
+                (g_to_relay if count == reach and j in relayed else g_copy)(a, j).start()
             gown[a, 0] = key_part[size - tok :]
             gown[a, 1] = value_part[size - tok :]
 
@@ -321,6 +389,15 @@
     for copy in stores:
         copy.start()
 
+    if relaying:
+
+        @pl.when(idx == reach)
+        def _():
+            for a in range(heads):
+                for j in relayed:
+                    g_to_relay(a, j).wait_recv()
+                    g_forward(a, j).start()
+
     for a in range(heads):
 
         def collect(j, _, a=a):
@@ -354,20 +431,54 @@
             g_copy(a, j).wait_send()
             return 0
 
-        lax.fori_loop(local + 1, after, end_kv, 0)
-        lax.fori_loop(0, local, end_g, 0)
-
-
-def hand_on(*refs):
-    count = len(refs) // 2
-    sems = refs[-1]
-    copies = [
-        pltpu.make_async_copy(refs[n], refs[count + n], sems.at[n]) for n in range(count)
-    ]
-    for copy in copies:
-        copy.start()
-    for copy in copies:
-        copy.wait()
+        for j in relayed:
+            pl.when(idx == j)(kv_to_relay(a, j).wait_send)
+        lax.fori_loop(local + 1, after - skip, end_kv, 0)
+        if not relaying:
+            lax.fori_loop(0, local, end_g, 0)
+            continue
+
+        @pl.when(idx != reach - 1)
+        def _(end_g=end_g):
+            lax.fori_loop(0, local, end_g, 0)
+
+        @pl.when(idx == reach - 1)
+        def _(a=a):
+            for j in range(reach - 1):
+                (g_to_relay if j in relayed else g_copy)(a, j).wait_send()
+
+        @pl.when(idx == reach)
+        def _(a=a):
+            for j in relayed:
+                kv_forward(a, j).wait_send()
+                g_forward(a, j).wait_send()
+
+
+def hand_on(pieces, *refs):
+    sources, targets, buffers = refs[0:4], refs[4:8], refs[8:12]
+    in_sem, out_sem = refs[12:]
+    copies = []
+    for n in range(4):
+        size = sources[n].shape[0] // pieces[n]
+        for m in range(pieces[n]):
+            part = pl.ds(m * size, size)
+            copies.append(
+                (
+                    pltpu.make_async_copy(
+                        sources[n].at[part], buffers[n].at[part], in_sem.at[n, m]
+                    ),
+                    pltpu.make_async_copy(
+                        buffers[n].at[part], targets[n].at[part], out_sem.at[n, m]
+                    ),
+                )
+            )
+    for first, _ in copies:
+        first.start()
+    for first, second in copies:
+        first.wait()
+        second.start()
+    for _, second in copies:
+        second.wait()
 
 
 def shards(query_rows, key_rows, value_rows, grad_out, lengths):
@@ -380,6 +491,7 @@
     docs = -(-lengths.shape[0] // 8) * 8
     wide = 2 if group % 2 == 0 else 1
     unrolled = reach <= UNROLLED
+    relays = reach if unrolled else 1
     held = reach * tok if unrolled else 16
     anywhere = pl.BlockSpec(memory_space=pl.ANY)
     vmem = pl.BlockSpec(memory_space=pltpu.VMEM)
@@ -401,10 +513,12 @@
         jax.ShapeDtypeStruct(key_rows.shape, bf16),
         jax.ShapeDtypeStruct(value_rows.shape, bf16),
     )
+    pieces = (4, 4, 1, 1) if tok % 64 == 0 else (1, 1, 1, 1)
     results = pl.pallas_call(
         functools.partial(kernel, devices),
         out_shape=shapes,
-        in_specs=[anywhere] * 4 + [pl.BlockSpec(memory_space=pltpu.SMEM)],
+        in_specs=[pl.BlockSpec(memory_space=pltpu.HBM)] * 4
+        + [pl.BlockSpec(memory_space=pltpu.SMEM)],
         out_specs=(anywhere, anywhere, vmem, vmem),
         scratch_shapes=[
             pltpu.VMEM((tok, width), bf16),
@@ -428,21 +542,30 @@
             dma((heads, reach)),
             dma((devices,)),
             dma((devices,)),
+            pltpu.VMEM((heads, relays, 2, tok, HD), bf16),
+            pltpu.VMEM((heads, relays, 2, tok, HD), bf16),
+            dma((heads,)),
+            dma((heads, relays)),
+            dma((heads, relays)),
+            dma((heads, relays)),
+            dma((heads, relays)),
+            dma((heads, relays)),
         ]
         + ([] if unrolled else loop_scratch),
         compiler_params=pltpu.CompilerParams(
-            collective_id=0, has_side_effects=True, vmem_limit_bytes=56 * 1024 * 1024
+            collective_id=0, has_side_effects=True, vmem_limit_bytes=(24 if unrolled else 56) * 1024 * 1024
         ),
         cost_estimate=pl.CostEstimate(
             flops=12 * pairs * HD, bytes_accessed=8 * tok * width, transcendentals=pairs
         ),
     )(query_rows, key_rows, value_rows, grad_out, lengths)
     return pl.pallas_call(
-        hand_on,
+        functools.partial(hand_on, pieces),
         out_shape=shapes,
         in_specs=[anywhere] * 4,
         out_specs=(anywhere,) * 4,
-        scratch_shapes=[dma((4,))],
+        scratch_shapes=[pltpu.VMEM(shape.shape, bf16) for shape in shapes]
+        + [dma((4, 4)), dma((4, 4))],
         cost_estimate=pl.CostEstimate(
             flops=0, bytes_accessed=8 * tok * width, transcendentals=0
         ),

time: 65.2 us -> 39.4 us (0.60)
  the two profiles are of different devices: /device:TPU:0 before, /device:TPU:4 now
where the time goes in v3:
time: 39.4 us; the launch traced here: 39 us
  Pallas kernels  31 us (79%)
  local copies, waits for them, and re-layouts  7.22 us (18%)
  between operations  0.82 us (2%)
    pallas_call x1, Pallas kernels, shards(): pl.pallas_call(functools.partial(kernel, devices), out_shape=shapes, in_s...  28.7 us
    unnamed x18, local copies, waits for them, and re-layouts  7.22 us
    pallas_call x1, Pallas kernels, shards(): pl.pallas_call(functools.partial(hand_on, pieces), out_shape=shapes, in_s...  2.26 us

profile of v3, /device:TPU:4, one launch (start us, length us, event | category | flops | bytes accessed | tf_op | source)
XLA Modules:
  0.0 39.0 jit_solution(14588666219280719222)
XLA Ops:
  0.6 0.0 copy-start.4
  0.6 1.0 %copy-done.4 = bf16[128,2048]{1,0:T(8,128)(2,1)S(1)} copy-done((bf16[128,2048]{1,0:T(8,128)(2,1)S(1)}, bf16[128,2048]{1,0:T(8,128)(2,1)}, u32[]{:S(2)}) %copy-start.4) | copy-done | bytes 524312
  1.7 0.0 copy-start.5
  1.7 1.0 %copy-done.5 = bf16[128,2048]{1,0:T(8,128)(2,1)S(1)} copy-done((bf16[128,2048]{1,0:T(8,128)(2,1)S(1)}, bf16[128,2048]{1,0:T(8,128)(2,1)}, u32[]{:S(2)}) %copy-start.5) | copy-done | bytes 524312
  2.7 0.0 copy-start.6
  2.7 0.8 %copy-done.6 = bf16[128,256]{1,0:T(8,128)(2,1)S(1)} copy-done((bf16[128,256]{1,0:T(8,128)(2,1)S(1)}, bf16[128,256]{1,0:T(8,128)(2,1)}, u32[]{:S(2)}) %copy-start.6) | copy-done | bytes 65560
  3.6 0.0 copy-start.7
  3.6 0.8 %copy-done.7 = bf16[128,256]{1,0:T(8,128)(2,1)S(1)} copy-done((bf16[128,256]{1,0:T(8,128)(2,1)S(1)}, bf16[128,256]{1,0:T(8,128)(2,1)}, u32[]{:S(2)}) %copy-start.7) | copy-done | bytes 65560
  4.4 0.0 copy-start.8
  4.4 0.7 %copy-done.8 = s32[4]{0:T(128)S(1)} copy-done((s32[4]{0:T(128)S(1)}, s32[4]{0:T(128)}, u32[]{:S(2)}) %copy-start.8) | copy-done | bytes 40
  5.1 28.7 %shard_map.84 = (bf16[128,2048]{1,0:T(8,128)(2,1)S(1)}, bf16[128,2048]{1,0:T(8,128)(2,1)S(1)}, bf16[128,256]{1,0:T(8,128)(2,1)S(1)}, bf16[128,256]{1,0:T(8,128)(2,1)S(1)}) custom-call(bf16[128,2048]{1,0:T(8,128)(2,1)S(1)} %copy-done.4, bf16[128,256]{1,0:T(8,128)(2,1)S(1)} %copy-done.6, bf16[128,256]{1,0:T(8,128)(2,1)S(1)} %copy-done.7, ...), custom_call_target="tpu_custom_call" | custom-call | flops 2013265920 | bytes 2097152 | tf_op jit(solution)/shard_map/pallas_call | solution.py:517
  33.8 0.0 copy-start
  33.8 0.8 %copy-done = bf16[128,2048]{1,0:T(8,128)(2,1)} copy-done((bf16[128,2048]{1,0:T(8,128)(2,1)}, bf16[128,2048]{1,0:T(8,128)(2,1)S(1)}, u32[]{:S(2)}) %copy-start) | copy-done | bytes 524312
  34.6 0.0 copy-start.1
  34.6 0.8 %copy-done.1 = bf16[128,2048]{1,0:T(8,128)(2,1)} copy-done((bf16[128,2048]{1,0:T(8,128)(2,1)}, bf16[128,2048]{1,0:T(8,128)(2,1)S(1)}, u32[]{:S(2)}) %copy-start.1) | copy-done | bytes 524312
  35.4 0.0 copy-start.2
  35.4 0.6 %copy-done.2 = bf16[128,256]{1,0:T(8,128)(2,1)} copy-done((bf16[128,256]{1,0:T(8,128)(2,1)}, bf16[128,256]{1,0:T(8,128)(2,1)S(1)}, u32[]{:S(2)}) %copy-start.2) | copy-done | bytes 65560
  36.0 0.0 copy-start.3
  36.0 0.6 %copy-done.3 = bf16[128,256]{1,0:T(8,128)(2,1)} copy-done((bf16[128,256]{1,0:T(8,128)(2,1)}, bf16[128,256]{1,0:T(8,128)(2,1)S(1)}, u32[]{:S(2)}) %copy-start.3) | copy-done | bytes 65560
  36.6 2.3 %shard_map.85 = (bf16[128,2048]{1,0:T(8,128)(2,1)}, bf16[128,2048]{1,0:T(8,128)(2,1)}, bf16[128,256]{1,0:T(8,128)(2,1)}, bf16[128,256]{1,0:T(8,128)(2,1)}) custom-call(bf16[128,2048]{1,0:T(8,128)(2,1)} %copy-done, bf16[128,2048]{1,0:T(8,128)(2,1)} %copy-done.1, bf16[128,256]{1,0:T(8,128)(2,1)} %copy-done.2, bf16[128,256]{1,0:T(8,128)(2,1)} %copy-done.3), custom_call_target="tpu_custom_call" | custom-call | bytes 2097152 | tf_op jit(solution)/shard_map/pallas_call | solution.py:562
Async XLA Ops:
  0.6 1.0 %copy-start.4 = (bf16[128,2048]{1,0:T(8,128)(2,1)S(1)}, bf16[128,2048]{1,0:T(8,128)(2,1)}, u32[]{:S(2)}) copy-start(bf16[128,2048]{1,0:T(8,128)(2,1)} %q_hbm.1) | copy-start | bytes 1572868
  1.7 1.0 %copy-start.5 = (bf16[128,2048]{1,0:T(8,128)(2,1)S(1)}, bf16[128,2048]{1,0:T(8,128)(2,1)}, u32[]{:S(2)}) copy-start(bf16[128,2048]{1,0:T(8,128)(2,1)} %g_hbm.1) | copy-start | bytes 1572868
  2.7 0.8 %copy-start.6 = (bf16[128,256]{1,0:T(8,128)(2,1)S(1)}, bf16[128,256]{1,0:T(8,128)(2,1)}, u32[]{:S(2)}) copy-start(bf16[128,256]{1,0:T(8,128)(2,1)} %k_hbm.1) | copy-start | bytes 196612
  3.6 0.8 %copy-start.7 = (bf16[128,256]{1,0:T(8,128)(2,1)S(1)}, bf16[128,256]{1,0:T(8,128)(2,1)}, u32[]{:S(2)}) copy-start(bf16[128,256]{1,0:T(8,128)(2,1)} %v_hbm.1) | copy-start | bytes 196612
  4.4 0.7 %copy-start.8 = (s32[4]{0:T(128)S(1)}, s32[4]{0:T(128)}, u32[]{:S(2)}) copy-start(s32[4]{0:T(128)} %len_ref.1) | copy-start | bytes 52
  33.8 0.8 %copy-start = (bf16[128,2048]{1,0:T(8,128)(2,1)}, bf16[128,2048]{1,0:T(8,128)(2,1)S(1)}, u32[]{:S(2)}) copy-start(bf16[128,2048]{1,0:T(8,128)(2,1)S(1)} %get-tuple-element.8.refs_0_) | copy-start | bytes 1572868
  34.6 0.8 %copy-start.1 = (bf16[128,2048]{1,0:T(8,128)(2,1)}, bf16[128,2048]{1,0:T(8,128)(2,1)S(1)}, u32[]{:S(2)}) copy-start(bf16[128,2048]{1,0:T(8,128)(2,1)S(1)} %get-tuple-element.9.refs_1_) | copy-start | bytes 1572868
  35.4 0.6 %copy-start.2 = (bf16[128,256]{1,0:T(8,128)(2,1)}, bf16[128,256]{1,0:T(8,128)(2,1)S(1)}, u32[]{:S(2)}) copy-start(bf16[128,256]{1,0:T(8,128)(2,1)S(1)} %get-tuple-element.10.refs_2_) | copy-start | bytes 196612
  36.0 0.6 %copy-start.3 = (bf16[128,256]{1,0:T(8,128)(2,1)}, bf16[128,256]{1,0:T(8,128)(2,1)S(1)}, u32[]{:S(2)}) copy-start(bf16[128,256]{1,0:T(8,128)(2,1)S(1)} %get-tuple-element.11.refs_3_) | copy-start | bytes 196612

commit v4 on v2

--- a/solution.py
+++ b/solution.py
@@ -23,9 +23,7 @@
 
 
 def stacked(ref, first, count):
-    return jnp.concatenate(
-        [ref[:, (first + h) * HD : (first + h + 1) * HD] for h in range(count)], axis=0
-    )
+    return ref[pl.ds(first, count)].reshape(count * ref.shape[1], HD)
 
 
 def kernel(
@@ -63,7 +61,7 @@
     *loop_refs,
 ):
     heads, reach, _, tok, _ = kv.shape
-    group = qbuf.shape[1] // HD // heads
+    group = qbuf.shape[0] // heads
     docs = len_ref.shape[0]
     scale = 1.0 / math.sqrt(HD)
     to_exp2 = scale * math.log2(math.e)
@@ -83,15 +81,28 @@
                     source.at[:, pl.ds(a * HD, HD)], kv.at[a, local, n], kv_sem.at[a, n]
                 )
             )
-    loads = []
-    for a in range(heads):
-        cols = pl.ds(a * group * HD, group * HD)
-        for n, (source, target) in enumerate(((q_hbm, qbuf), (g_hbm, gbuf))):
-            loads.append(
-                pltpu.make_async_copy(source.at[:, cols], target.at[:, cols], load_sem.at[a, n])
-            )
-    for copy in own + loads:
+    for copy in own:
         copy.start()
+
+    def load(n, head):
+        source, target = ((q_hbm, qbuf), (g_hbm, gbuf))[n]
+        cols = pl.ds(pl.multiple_of(head * HD, HD), HD)
+        return pltpu.make_async_copy(source.at[:, cols], target.at[head], load_sem.at[n, head])
+
+    def save(n, head):
+        source, target = ((ostage, att_hbm), (qstage, gq_hbm))[n]
+        cols = pl.ds(pl.multiple_of(head * HD, HD), HD)
+        return pltpu.make_async_copy(source.at[head], target.at[:, cols], store_sem.at[n, head])
+
+    def for_heads(first, count, do):
+        def step(head, _):
+            do(0, head)
+            do(1, head)
+            return 0
+
+        lax.fori_loop(first, first + count, step, 0)
+
+    for_heads(0, heads * group, lambda n, head: load(n, head).start())
 
     barrier = pltpu.get_barrier_semaphore()
 
@@ -191,16 +202,17 @@
         key_index = lax.broadcasted_iota(jnp.int32, (size, wide * tok), 0)
         query_index = lax.rem(lax.broadcasted_iota(jnp.int32, (tok, wide * tok), 1), tok)
         causal = lax.broadcasted_iota(jnp.int32, (tok, wide * tok), 0) <= query_index
-        for a in range(heads):
+
+        def one_head(a, _):
             for j in range(count - 1):
                 arrival(kv.at[a, j], kv_recv.at[a, j]).wait_recv()
-            loads[2 * a].wait()
-            loads[2 * a + 1].wait()
+            for_heads(a * group, group, lambda n, head: load(n, head).wait())
             keys = kv[a, 0:count, 0].reshape(size, HD)
             values = kv[a, 0:count, 1].reshape(size, HD)
             keys_t = keys.T
             values_t = values.T
-            for p in range(group // wide):
+
+            def one_part(p, _):
                 first = a * group + p * wide
                 queries = stacked(qbuf, first, wide)
                 cotangents = stacked(gbuf, first, wide)
@@ -217,16 +229,18 @@
                 prob = expo * inverse
                 prob_low = prob.astype(jnp.bfloat16)
                 dscore = (prob * (dprob - delta)).astype(jnp.bfloat16)
-                wide_cols = slice(p * wide * tok, (p + 1) * wide * tok)
-                probs[0:size, wide_cols] = prob_low
-                dscores[0:size, wide_cols] = dscore
+                cols = pl.ds(pl.multiple_of(p * wide * tok, wide * tok), wide * tok)
+                probs[0:size, cols] = prob_low
+                dscores[0:size, cols] = dscore
                 out = dot_nn(values_t, prob_low)
                 grad = scale * dot_nn(keys_t, dscore)
                 for h in range(wide):
-                    cols = slice((first + h) * HD, (first + h + 1) * HD)
                     part = slice(h * tok, (h + 1) * tok)
-                    ostage[:, cols] = out[:, part].T.astype(jnp.bfloat16)
-                    qstage[:, cols] = grad[:, part].T.astype(jnp.bfloat16)
+                    ostage[first + h] = out[:, part].T.astype(jnp.bfloat16)
+                    qstage[first + h] = grad[:, part].T.astype(jnp.bfloat16)
+                return 0
+
+            lax.fori_loop(0, group // wide, one_part, 0, unroll=2 if group // wide % 2 == 0 else 1)
             key_part = dot_nn(dscores[0:size, :], stacked(qbuf, a * group, group))
             value_part = dot_nn(probs[0:size, :], stacked(gbuf, a * group, group))
             for j in range(count - 1):
@@ -236,13 +250,16 @@
                 g_copy(a, j).start()
             gown[a, 0] = key_part[size - tok :]
             gown[a, 1] = value_part[size - tok :]
+            for_heads(a * group, group, lambda n, head: save(n, head).start())
+            return 0
+
+        lax.fori_loop(0, heads, one_head, 0)
 
     def any_count(sbuf, dbuf, oacc, qacc, rowmax, rowsum, delta):
         key_index = lax.broadcasted_iota(jnp.int32, (tok, tok), 0)
         query_index = lax.broadcasted_iota(jnp.int32, (tok, tok), 1)
         for a in range(heads):
-            loads[2 * a].wait()
-            loads[2 * a + 1].wait()
+            for_heads(a * group, group, lambda n, head: load(n, head).wait())
             queries = stacked(qbuf, a * group, group)
             cotangents = stacked(gbuf, a * group, group)
             rowmax[...] = jnp.full(rowmax.shape, NEGATIVE, jnp.float32)
@@ -303,10 +320,10 @@
             lax.fori_loop(0, local, third_step, 0)
             gown[a, 0], gown[a, 1] = third_pass(local)
             for h in range(group):
-                cols = slice((a * group + h) * HD, (a * group + h + 1) * HD)
                 part = slice(h * tok, (h + 1) * tok)
-                ostage[:, cols] = oacc[:, part].T.astype(jnp.bfloat16)
-                qstage[:, cols] = (scale * qacc[:, part]).T.astype(jnp.bfloat16)
+                ostage[a * group + h] = oacc[:, part].T.astype(jnp.bfloat16)
+                qstage[a * group + h] = (scale * qacc[:, part]).T.astype(jnp.bfloat16)
+            for_heads(a * group, group, lambda n, head: save(n, head).start())
 
     if loop_refs:
         any_count(*loop_refs)
@@ -314,13 +331,6 @@
         for count in range(1, reach + 1):
             pl.when(local + 1 == count)(functools.partial(one_count, count))
 
-    stores = [
-        pltpu.make_async_copy(ostage, att_hbm, store_sem.at[0]),
-        pltpu.make_async_copy(qstage, gq_hbm, store_sem.at[1]),
-    ]
-    for copy in stores:
-        copy.start()
-
     for a in range(heads):
 
         def collect(j, _, a=a):
@@ -333,8 +343,7 @@
         gk_ref[:, cols] = (scale * gown[a, 0]).astype(jnp.bfloat16)
         gv_ref[:, cols] = gown[a, 1].astype(jnp.bfloat16)
 
-    for copy in stores:
-        copy.wait()
+    for_heads(0, heads * group, lambda n, head: save(n, head).wait())
 
     def end_l(target, _):
         @pl.when(target != idx)
@@ -358,16 +367,31 @@
         lax.fori_loop(0, local, end_g, 0)
 
 
-def hand_on(*refs):
-    count = len(refs) // 2
-    sems = refs[-1]
-    copies = [
-        pltpu.make_async_copy(refs[n], refs[count + n], sems.at[n]) for n in range(count)
-    ]
-    for copy in copies:
-        copy.start()
-    for copy in copies:
-        copy.wait()
+def hand_on(pieces, *refs):
+    sources, targets, buffers = refs[0:4], refs[4:8], refs[8:12]
+    in_sem, out_sem = refs[12:]
+    copies = []
+    for n in range(4):
+        size = sources[n].shape[0] // pieces[n]
+        for m in range(pieces[n]):
+            part = pl.ds(m * size, size)
+            copies.append(
+                (
+                    pltpu.make_async_copy(
+                        sources[n].at[part], buffers[n].at[part], in_sem.at[n, m]
+                    ),
+                    pltpu.make_async_copy(
+                        buffers[n].at[part], targets[n].at[part], out_sem.at[n, m]
+                    ),
+                )
+            )
+    for first, _ in copies:
+        first.start()
+    for first, second in copies:
+        first.wait()
+        second.start()
+    for _, second in copies:
+        second.wait()
 
 
 def shards(query_rows, key_rows, value_rows, grad_out, lengths):
@@ -401,27 +425,28 @@
         jax.ShapeDtypeStruct(key_rows.shape, bf16),
         jax.ShapeDtypeStruct(value_rows.shape, bf16),
     )
+    pieces = (4, 4, 1, 1) if tok % 64 == 0 else (1, 1, 1, 1)
     results = pl.pallas_call(
         functools.partial(kernel, devices),
         out_shape=shapes,
         in_specs=[anywhere] * 4 + [pl.BlockSpec(memory_space=pltpu.SMEM)],
         out_specs=(anywhere, anywhere, vmem, vmem),
         scratch_shapes=[
-            pltpu.VMEM((tok, width), bf16),
-            pltpu.VMEM((tok, width), bf16),
+            pltpu.VMEM((heads * group, tok, HD), bf16),
+            pltpu.VMEM((heads * group, tok, HD), bf16),
             pltpu.VMEM((heads, reach, 2, tok, HD), bf16),
             pltpu.VMEM((held, rows), bf16),
             pltpu.VMEM((held, rows), bf16),
-            pltpu.VMEM((tok, width), bf16),
-            pltpu.VMEM((tok, width), bf16),
+            pltpu.VMEM((heads * group, tok, HD), bf16),
+            pltpu.VMEM((heads * group, tok, HD), bf16),
             pltpu.VMEM((heads, reach, 2, tok, HD), bf16),
             pltpu.VMEM((heads, reach, 2, tok, HD), bf16),
             pltpu.VMEM((heads, 2, tok, HD), f32),
             pltpu.VMEM((devices, docs, HD), jnp.int32),
             pltpu.VMEM((1, wide * tok), jnp.int32),
+            dma((2, heads * group)),
             dma((heads, 2)),
-            dma((heads, 2)),
-            dma((2,)),
+            dma((2, heads * group)),
             dma((heads, reach)),
             dma((heads, reach)),
             dma((heads, reach)),
@@ -438,11 +463,12 @@
         ),
     )(query_rows, key_rows, value_rows, grad_out, lengths)
     return pl.pallas_call(
-        hand_on,
+        functools.partial(hand_on, pieces),
         out_shape=shapes,
         in_specs=[anywhere] * 4,
         out_specs=(anywhere,) * 4,
-        scratch_shapes=[dma((4,))],
+        scratch_shapes=[pltpu.VMEM(shape.shape, bf16) for shape in shapes]
+        + [dma((4, 4)), dma((4, 4))],
         cost_estimate=pl.CostEstimate(
             flops=0, bytes_accessed=8 * tok * width, transcendentals=0
         ),

time: 65.2 us -> 32.1 us (0.49)
  Pallas kernels: 64.2 us -> 31.3 us
    pallas_call x1, Pallas kernels: 36.9 us -> 2.27 us  [shards(): pl.pallas_call(functools.partial(hand_on, pieces), out_shape=shapes, in_s...]
    pallas_call x1, Pallas kernels: 27.4 us -> 29 us  [shards(): pl.pallas_call(functools.partial(kernel, devices), out_shape=shapes, in_s...]
where the time goes in v4:
time: 32.1 us; the launch traced here: 31.9 us
  Pallas kernels  31.3 us (98%)
  between operations  0.64 us (2%)
    pallas_call x1, Pallas kernels, shards(): pl.pallas_call(functools.partial(kernel, devices), out_shape=shapes, in_s...  29 us
    pallas_call x1, Pallas kernels, shards(): pl.pallas_call(functools.partial(hand_on, pieces), out_shape=shapes, in_s...  2.27 us

profile of v4, /device:TPU:0, one launch (start us, length us, event | category | flops | bytes accessed | tf_op | source)
XLA Modules:
  0.0 31.9 jit_solution(14072488156722380356)
XLA Ops:
  0.6 29.0 %shard_map.84 = (bf16[128,2048]{1,0:T(8,128)(2,1)}, bf16[128,2048]{1,0:T(8,128)(2,1)}, bf16[128,256]{1,0:T(8,128)(2,1)}, bf16[128,256]{1,0:T(8,128)(2,1)}) custom-call(bf16[128,2048]{1,0:T(8,128)(2,1)} %q_hbm.1, bf16[128,256]{1,0:T(8,128)(2,1)} %k_hbm.1, bf16[128,256]{1,0:T(8,128)(2,1)} %v_hbm.1, bf16[128,2048]{1,0:T(8,128)(2,1)} %g_hbm.1, s32[4]{0:T(128)} %len_ref.1), custom_call_target="tpu_custom_call" | custom-call | flops 2013265920 | bytes 2097152 | tf_op jit(solution)/shard_map/pallas_call | solution.py:429
  29.6 2.3 %shard_map.85 = (bf16[128,2048]{1,0:T(8,128)(2,1)}, bf16[128,2048]{1,0:T(8,128)(2,1)}, bf16[128,256]{1,0:T(8,128)(2,1)}, bf16[128,256]{1,0:T(8,128)(2,1)}) custom-call(bf16[128,2048]{1,0:T(8,128)(2,1)} %get-tuple-element.8.refs_0_, bf16[128,2048]{1,0:T(8,128)(2,1)} %get-tuple-element.9.refs_1_, bf16[128,256]{1,0:T(8,128)(2,1)} %get-tuple-element.10.refs_2_, ...), custom_call_target="tpu_custom_call" | custom-call | bytes 2097152 | tf_op jit(solution)/shard_map/pallas_call | solution.py:465

commit v5 on v2

--- a/solution.py
+++ b/solution.py
@@ -220,13 +220,13 @@
                 wide_cols = slice(p * wide * tok, (p + 1) * wide * tok)
                 probs[0:size, wide_cols] = prob_low
                 dscores[0:size, wide_cols] = dscore
-                out = dot_nn(values_t, prob_low)
-                grad = scale * dot_nn(keys_t, dscore)
+                out = dot_nn(values_t, prob_low).astype(jnp.bfloat16).T
+                grad = (scale * dot_nn(keys_t, dscore)).astype(jnp.bfloat16).T
                 for h in range(wide):
                     cols = slice((first + h) * HD, (first + h + 1) * HD)
                     part = slice(h * tok, (h + 1) * tok)
-                    ostage[:, cols] = out[:, part].T.astype(jnp.bfloat16)
-                    qstage[:, cols] = grad[:, part].T.astype(jnp.bfloat16)
+                    ostage[:, cols] = out[part]
+                    qstage[:, cols] = grad[part]
             key_part = dot_nn(dscores[0:size, :], stacked(qbuf, a * group, group))
             value_part = dot_nn(probs[0:size, :], stacked(gbuf, a * group, group))
             for j in range(count - 1):
@@ -358,16 +358,31 @@
         lax.fori_loop(0, local, end_g, 0)
 
 
-def hand_on(*refs):
-    count = len(refs) // 2
-    sems = refs[-1]
-    copies = [
-        pltpu.make_async_copy(refs[n], refs[count + n], sems.at[n]) for n in range(count)
-    ]
-    for copy in copies:
-        copy.start()
-    for copy in copies:
-        copy.wait()
+def hand_on(pieces, *refs):
+    sources, targets, buffers = refs[0:4], refs[4:8], refs[8:12]
+    in_sem, out_sem = refs[12:]
+    copies = []
+    for n in range(4):
+        size = sources[n].shape[0] // pieces[n]
+        for m in range(pieces[n]):
+            part = pl.ds(m * size, size)
+            copies.append(
+                (
+                    pltpu.make_async_copy(
+                        sources[n].at[part], buffers[n].at[part], in_sem.at[n, m]
+                    ),
+                    pltpu.make_async_copy(
+                        buffers[n].at[part], targets[n].at[part], out_sem.at[n, m]
+                    ),
+                )
+            )
+    for first, _ in copies:
+        first.start()
+    for first, second in copies:
+        first.wait()
+        second.start()
+    for _, second in copies:
+        second.wait()
 
 
 def shards(query_rows, key_rows, value_rows, grad_out, lengths):
@@ -401,6 +416,7 @@
         jax.ShapeDtypeStruct(key_rows.shape, bf16),
         jax.ShapeDtypeStruct(value_rows.shape, bf16),
     )
+    pieces = (4, 4, 1, 1) if tok % 64 == 0 else (1, 1, 1, 1)
     results = pl.pallas_call(
         functools.partial(kernel, devices),
         out_shape=shapes,
@@ -438,11 +454,12 @@
         ),
     )(query_rows, key_rows, value_rows, grad_out, lengths)
     return pl.pallas_call(
-        hand_on,
+        functools.partial(hand_on, pieces),
         out_shape=shapes,
         in_specs=[anywhere] * 4,
         out_specs=(anywhere,) * 4,
-        scratch_shapes=[dma((4,))],
+        scratch_shapes=[pltpu.VMEM(shape.shape, bf16) for shape in shapes]
+        + [dma((4, 4)), dma((4, 4))],
         cost_estimate=pl.CostEstimate(
             flops=0, bytes_accessed=8 * tok * width, transcendentals=0
         ),

time: 65.2 us -> 30.6 us (0.47)
  Pallas kernels: 64.2 us -> 29.6 us
    pallas_call x1, Pallas kernels: 36.9 us -> 2.27 us  [shards(): pl.pallas_call(functools.partial(hand_on, pieces), out_shape=shapes, in_s...]
where the time goes in v5:
time: 30.6 us; the launch traced here: 30.4 us
  Pallas kernels  29.6 us (97%)
  between operations  0.8 us (3%)
    pallas_call x1, Pallas kernels, shards(): pl.pallas_call(functools.partial(kernel, devices), out_shape=shapes, in_s...  27.4 us
    pallas_call x1, Pallas kernels, shards(): pl.pallas_call(functools.partial(hand_on, pieces), out_shape=shapes, in_s...  2.27 us

profile of v5, /device:TPU:0, one launch (start us, length us, event | category | flops | bytes accessed | tf_op | source)
XLA Modules:
  0.0 30.4 jit_solution(17163323505361394451)
XLA Ops:
  0.6 27.4 %shard_map.84 = (bf16[128,2048]{1,0:T(8,128)(2,1)}, bf16[128,2048]{1,0:T(8,128)(2,1)}, bf16[128,256]{1,0:T(8,128)(2,1)}, bf16[128,256]{1,0:T(8,128)(2,1)}) custom-call(bf16[128,2048]{1,0:T(8,128)(2,1)} %q_hbm.1, bf16[128,256]{1,0:T(8,128)(2,1)} %k_hbm.1, bf16[128,256]{1,0:T(8,128)(2,1)} %v_hbm.1, bf16[128,2048]{1,0:T(8,128)(2,1)} %g_hbm.1, s32[4]{0:T(128)} %len_ref.1), custom_call_target="tpu_custom_call" | custom-call | flops 2013265920 | bytes 2097152 | tf_op jit(solution)/shard_map/pallas_call | solution.py:420
  28.0 2.3 %shard_map.85 = (bf16[128,2048]{1,0:T(8,128)(2,1)}, bf16[128,2048]{1,0:T(8,128)(2,1)}, bf16[128,256]{1,0:T(8,128)(2,1)}, bf16[128,256]{1,0:T(8,128)(2,1)}) custom-call(bf16[128,2048]{1,0:T(8,128)(2,1)} %get-tuple-element.8.refs_0_, bf16[128,2048]{1,0:T(8,128)(2,1)} %get-tuple-element.9.refs_1_, bf16[128,256]{1,0:T(8,128)(2,1)} %get-tuple-element.10.refs_2_, ...), custom_call_target="tpu_custom_call" | custom-call | bytes 2097152 | tf_op jit(solution)/shard_map/pallas_call | solution.py:456

commit v6 on v5

--- a/solution.py
+++ b/solution.py
@@ -67,7 +67,7 @@
     docs = len_ref.shape[0]
     scale = 1.0 / math.sqrt(HD)
     to_exp2 = scale * math.log2(math.e)
-    wide = 2 if group % 2 == 0 else 1
+    wide = 4 if group % 4 == 0 else 1
 
     idx = lax.axis_index("seq")
     in_first = idx < reach
@@ -393,7 +393,7 @@
     reach = devices // 2 + 1
     rows = group * tok
     docs = -(-lengths.shape[0] // 8) * 8
-    wide = 2 if group % 2 == 0 else 1
+    wide = 4 if group % 4 == 0 else 1
     unrolled = reach <= UNROLLED
     held = reach * tok if unrolled else 16
     anywhere = pl.BlockSpec(memory_space=pl.ANY)

time: 30.6 us -> 30 us (0.980)
  Pallas kernels: 29.6 us -> 29.1 us
    pallas_call x1, Pallas kernels: 27.4 us -> 26.8 us  [shards(): pl.pallas_call(functools.partial(kernel, devices), out_shape=shapes, in_s...]
where the time goes in v6:
time: 30 us; the launch traced here: 29.9 us
  Pallas kernels  29.1 us (97%)
  between operations  0.8 us (3%)
    pallas_call x1, Pallas kernels, shards(): pl.pallas_call(functools.partial(kernel, devices), out_shape=shapes, in_s...  26.8 us
    pallas_call x1, Pallas kernels, shards(): pl.pallas_call(functools.partial(hand_on, pieces), out_shape=shapes, in_s...  2.27 us

profile of v6, /device:TPU:0, one launch (start us, length us, event | category | flops | bytes accessed | tf_op | source)
XLA Modules:
  0.0 29.9 jit_solution(15061404104418165925)
XLA Ops:
  0.6 26.8 %shard_map.84 = (bf16[128,2048]{1,0:T(8,128)(2,1)}, bf16[128,2048]{1,0:T(8,128)(2,1)}, bf16[128,256]{1,0:T(8,128)(2,1)}, bf16[128,256]{1,0:T(8,128)(2,1)}) custom-call(bf16[128,2048]{1,0:T(8,128)(2,1)} %q_hbm.1, bf16[128,256]{1,0:T(8,128)(2,1)} %k_hbm.1, bf16[128,256]{1,0:T(8,128)(2,1)} %v_hbm.1, bf16[128,2048]{1,0:T(8,128)(2,1)} %g_hbm.1, s32[4]{0:T(128)} %len_ref.1), custom_call_target="tpu_custom_call" | custom-call | flops 2013265920 | bytes 2097152 | tf_op jit(solution)/shard_map/pallas_call | solution.py:420
  27.4 2.3 %shard_map.85 = (bf16[128,2048]{1,0:T(8,128)(2,1)}, bf16[128,2048]{1,0:T(8,128)(2,1)}, bf16[128,256]{1,0:T(8,128)(2,1)}, bf16[128,256]{1,0:T(8,128)(2,1)}) custom-call(bf16[128,2048]{1,0:T(8,128)(2,1)} %get-tuple-element.8.refs_0_, bf16[128,2048]{1,0:T(8,128)(2,1)} %get-tuple-element.9.refs_1_, bf16[128,256]{1,0:T(8,128)(2,1)} %get-tuple-element.10.refs_2_, ...), custom_call_target="tpu_custom_call" | custom-call | bytes 2097152 | tf_op jit(solution)/shard_map/pallas_call | solution.py:456
